TPU v7x, 128 devices: a whole 4x4x4 slice. The times are simulated.
128 devices in a mesh: dp: 8 (over x, core), fsdp: 16 (over y, z).
Axes of the slice: x: 4, y: 4, z: 4, core: 2. Of those that a mesh axis runs over, the one named last changes fastest.
Arguments:
- grad_parts: bfloat16 [8, 8192, 14336], P('dp', 'fsdp'), may hold values from -8 to 8
- weight: bfloat16 [8192, 14336], P('fsdp', 'dp'), may hold values from -6 to 6
- projector: float32 [8192, 512], P('fsdp'), may hold values from -0.0625 to 0.0625
- exp_avg: float32 [512, 14336], P('fsdp', 'dp'), may hold values from -4 to 4
- exp_avg_sq: float32 [512, 14336], P('fsdp', 'dp'), may hold values from 0.1 to 1
Outputs:
- new_weight: bfloat16 [8192, 14336], P('fsdp', 'dp')
- new_projector: float32 [8192, 512], P('fsdp')
- moment_one: float32 [512, 14336], P('fsdp', 'dp')
- moment_two: float32 [512, 14336], P('fsdp', 'dp')
All inputs are finite; a program needn't handle non-finite values.
Results may differ from a plain program's by a relative error of at most 0.009.
Values may be sent and summed in bfloat16 or wider, within the bound.
A program may use at most 128 MiB of HBM per device.

v0:
```python
import jax
import jax.numpy as jnp
from jax import lax
from jax.sharding import PartitionSpec as P

NS_ITERS = 5


COEF_A = 3.4445
COEF_B = -4.775
COEF_C = 2.0315


def adam_step(low_share, exp_avg, exp_avg_sq):
    moment_one = 0.9 * exp_avg + 0.1 * low_share
    moment_two = 0.999 * exp_avg_sq + 0.001 * low_share * low_share
    normed = moment_one / (jnp.sqrt(moment_two) + 1e-08)
    return (moment_one, moment_two, normed)


def matmul(left, right):
    return jnp.dot(left, right, precision=lax.Precision.HIGHEST, preferred_element_type=jnp.float32)


def polynomial_of(gram, identity):
    return COEF_A * identity + COEF_B * gram + COEF_C * matmul(gram, gram)


def on_device(grad_parts, weight, projector, exp_avg, exp_avg_sq):
    grad_total = lax.psum_scatter(
        grad_parts[0].astype(jnp.float32).astype(jnp.bfloat16),
        "dp",
        scatter_dimension=1,
        tiled=True,
    ).astype(jnp.float32)
    share_rows = exp_avg.shape[0]
    first_row = lax.axis_index("fsdp") * share_rows
    low_rank = lax.psum(matmul(projector.T, grad_total), "fsdp")
    low_share = lax.dynamic_slice_in_dim(low_rank, first_row, share_rows, 0)
    moment_one, moment_two, normed_share = adam_step(low_share, exp_avg, exp_avg_sq)
    normed = lax.all_gather(normed_share, "fsdp", axis=0, tiled=True)
    new_weight = (weight.astype(jnp.float32) - 2.0 * matmul(projector, normed)).astype(jnp.bfloat16)
    residual = grad_total - matmul(projector, low_rank)
    tangent = lax.psum(matmul(residual, low_rank.T), "dp")
    rank_size = projector.shape[1]
    identity = jnp.eye(rank_size, dtype=jnp.float32)
    tangent_sq = lax.psum(jnp.sum(tangent * tangent), "fsdp")
    tan_scale = 0.5 * jnp.sqrt(jnp.float32(rank_size)) / jnp.sqrt(tangent_sq + 1e-06)
    frame = projector + tan_scale * tangent
    frame_sq = lax.psum(jnp.sum(frame * frame), "fsdp")
    new_projector = frame / jnp.sqrt(frame_sq + 1e-06)
    for sweep in range(NS_ITERS):
        gram_now = lax.psum(matmul(new_projector.T, new_projector), "fsdp")
        new_projector = matmul(new_projector, polynomial_of(gram_now, identity))
    return (new_weight, new_projector, moment_one, moment_two)


def solution(mesh):
    return jax.shard_map(
        on_device,
        mesh=mesh,
        in_specs=(
            P("dp", "fsdp", None),
            P("fsdp", "dp"),
            P("fsdp", None),
            P("fsdp", "dp"),
            P("fsdp", "dp"),
        ),
        out_specs=(P("fsdp", "dp"), P("fsdp", None), P("fsdp", "dp"), P("fsdp", "dp")),
        check_vma=False,
    )
```

profile of v0, /device:TPU:1, one launch (start us, length us, event | category | flops | bytes accessed | tf_op | source)
XLA Modules:
  0.0 901.1 jit_solution(15470891800430087564)
XLA Ops:
  7.9 87.5 %reduce-scatter.2.cloned.1.call-done = bf16[512,1792]{1,0:T(8,128)(2,1)} async-done(((bf16[512,14336]{1,0:T(8,128)(2,1)}), bf16[512,1792]{1,0:T(8,128)(2,1)}) %reduce-scatter.2.cloned.1.call-update) | async-done | bytes 1835024 | tf_op jit(solution)/shard_map/reduce_scatter | solution.py:30
  95.4 6.4 fusion.12
  102.1 98.8 %all-reduce.8.cloned.1.call-done = f32[512,1792]{1,0:T(8,128)} async-done(((f32[512,1792]{1,0:T(8,128)}), f32[512,1792]{1,0:T(8,128)}) %all-reduce.8.cloned.1.call-update) | async-done | bytes 3670032 | tf_op jit(solution)/shard_map/psum | solution.py:38
  200.9 9.1 %fusion.13 = f32[1792,512]{0,1:T(8,128)S(1)} fusion(f32[512,1792]{1,0:T(8,128)} %all-reduce.8.cloned.1.call-done, f32[512,512]{1,0:T(8,128)S(1)} %copy-done.1), kind=kOutput, calls=%fused_computation.32 | convolution fusion | flops 5637144576 | bytes 8388608 | tf_op jit(solution)/shard_map/dot_general | solution.py:22
  210.0 7.2 fusion
  217.3 60.0 %all-reduce.10.cloned.1.call-done = f32[512,512]{1,0:T(8,128)} async-done(((f32[512,512]{1,0:T(8,128)}), f32[512,512]{1,0:T(8,128)}) %all-reduce.10.cloned.1.call-update) | async-done | bytes 1048592 | tf_op jit(solution)/shard_map/psum | solution.py:44
  279.4 34.1 %psum.65 = f32[]{:T(128)} all-reduce(f32[]{:T(128)} %multiply_reduce_fusion.1), channel_id=1, replica_groups=mesh['dp'=8,'fsdp'=16] {'fsdp'}, use_global_device_ids=true, to_apply=%region_4.0 | all-reduce | flops 1 | bytes 8 | tf_op jit(solution)/shard_map/psum | solution.py:47
  316.3 29.4 %psum.66 = f32[]{:T(128)} all-reduce(f32[]{:T(128)} %get-tuple-element.8), channel_id=1, replica_groups=mesh['dp'=8,'fsdp'=16] {'fsdp'}, use_global_device_ids=true, to_apply=%region_6.0 | all-reduce | flops 1 | bytes 8 | tf_op jit(solution)/shard_map/psum | solution.py:50
  346.4 2.9 fusion.9
  349.4 97.1 %all-reduce.12.cloned.1.call-done = f32[512,512]{1,0:T(8,128)} async-done(((f32[512,512]{1,0:T(8,128)}), f32[512,512]{1,0:T(8,128)}) %all-reduce.12.cloned.1.call-update) | async-done | bytes 1048592 | tf_op jit(solution)/shard_map/psum | solution.py:53
  446.4 3.8 fusion.7
  455.5 85.9 %all-reduce.14.cloned.1.call-done = f32[512,512]{1,0:T(8,128)} async-done(((f32[512,512]{1,0:T(8,128)}), f32[512,512]{1,0:T(8,128)}) %all-reduce.14.cloned.1.call-update) | async-done | bytes 1048592 | tf_op jit(solution)/shard_map/psum | solution.py:53
  541.4 3.8 fusion.6
  547.1 2.8 fusion.16
  550.0 86.3 %all-reduce.16.cloned.1.call-done = f32[512,512]{1,0:T(8,128)} async-done(((f32[512,512]{1,0:T(8,128)}), f32[512,512]{1,0:T(8,128)}) %all-reduce.16.cloned.1.call-update) | async-done | bytes 1048592 | tf_op jit(solution)/shard_map/psum | solution.py:53
  636.4 3.8 fusion.5
  645.1 86.2 %all-reduce.18.cloned.1.call-done = f32[512,512]{1,0:T(8,128)} async-done(((f32[512,512]{1,0:T(8,128)}), f32[512,512]{1,0:T(8,128)}) %all-reduce.18.cloned.1.call-update) | async-done | bytes 1048592 | tf_op jit(solution)/shard_map/psum | solution.py:53
  731.3 3.8 fusion.4
  737.0 2.8 fusion.20
  741.8 3.8 copy.9
  745.6 80.6 %all-reduce.20.cloned.1.call-done = f32[512,512]{1,0:T(8,128)} async-done(((f32[512,512]{1,0:T(8,128)}), f32[512,512]{1,0:T(8,128)}) %all-reduce.20.cloned.1.call-update) | async-done | bytes 1048592 | tf_op jit(solution)/shard_map/psum | solution.py:53
  826.2 3.8 fusion.3
  832.9 45.6 %all-gather.2.cloned.1.call-done = f32[512,1792]{1,0:T(8,128)} async-done(((f32[32,1792]{1,0:T(8,128)}), f32[512,1792]{1,0:T(8,128)}) %all-gather.2.cloned.1.call-update) | async-done | bytes 3670032 | tf_op jit(solution)/shard_map/all_gather | solution.py:41
  878.5 13.5 %fusion.1 = bf16[512,1792]{0,1:T(8,128)(2,1)S(1)} fusion(bf16[512,1792]{0,1:T(8,128)(2,1)} %copy.9, f32[512,1792]{1,0:T(8,128)} %all-gather.2.cloned.1.call-done, f32[512,512]{1,0:T(8,128)S(1)} %copy-done.1), kind=kOutput, calls=%fused_computation.3 | convolution fusion | flops 5640814592 | bytes 8388608 | tf_op jit(solution)/shard_map/dot_general | solution.py:22
  (39 shorter events, 26.4 us)
Async XLA Ops:
  7.2 88.3 %reduce-scatter.2.cloned.1.call-start = ((), (), s32[]{:S(2)}) async-start(), calls=%async_computation.1 | async-start | bytes 16515072 | tf_op jit(solution)/shard_map/reduce_scatter | solution.py:30
  7.2 88.2 %copy-start.1 = (f32[512,512]{1,0:T(8,128)S(1)}, f32[512,512]{1,0:T(8,128)}, u32[]{:S(2)}) copy-start(f32[512,512]{1,0:T(8,128)} %param.7) | copy-start | bytes 3145732
  7.9 193.0 %all-reduce.8.cloned.1.call-start = ((), (), s32[]{:S(2)}) async-start(), calls=%async_computation.2 | async-start | bytes 7340032 | tf_op jit(solution)/shard_map/psum | solution.py:38
  101.9 108.2 %copy-start.2 = (bf16[512,1792]{1,0:T(8,128)(2,1)S(1)}, bf16[512,1792]{1,0:T(8,128)(2,1)}, u32[]{:S(2)}) copy-start(bf16[512,1792]{1,0:T(8,128)(2,1)} %reduce-scatter.2.cloned.1.call-done) | copy-start | bytes 5505028
  101.9 175.5 %all-reduce.10.cloned.1.call-start = ((), (), s32[]{:S(2)}) async-start(), calls=%async_computation.4 | async-start | bytes 2097152 | tf_op jit(solution)/shard_map/psum | solution.py:44
  200.9 9.1 %copy-start = (f32[512,1792]{1,0:T(8,128)S(1)}, f32[512,1792]{1,0:T(8,128)}, u32[]{:S(2)}) copy-start(f32[512,1792]{1,0:T(8,128)} %all-reduce.8.cloned.1.call-done) | copy-start | bytes 11010052
  217.3 229.2 %all-reduce.12.cloned.1.call-start = ((), (), s32[]{:S(2)}) async-start(), calls=%async_computation.5 | async-start | bytes 2097152 | tf_op jit(solution)/shard_map/psum | solution.py:53
  349.3 192.1 %all-reduce.14.cloned.1.call-start = ((), (), s32[]{:S(2)}) async-start(), calls=%async_computation.6 | async-start | bytes 2097152 | tf_op jit(solution)/shard_map/psum | solution.py:53
  455.0 181.4 %all-reduce.16.cloned.1.call-start = ((), (), s32[]{:S(2)}) async-start(), calls=%async_computation.7 | async-start | bytes 2097152 | tf_op jit(solution)/shard_map/psum | solution.py:53
  550.0 181.3 %all-reduce.18.cloned.1.call-start = ((), (), s32[]{:S(2)}) async-start(), calls=%async_computation.8 | async-start | bytes 2097152 | tf_op jit(solution)/shard_map/psum | solution.py:53
  644.9 181.3 %all-reduce.20.cloned.1.call-start = ((), (), s32[]{:S(2)}) async-start(), calls=%async_computation.9 | async-start | bytes 2097152 | tf_op jit(solution)/shard_map/psum | solution.py:53
  735.1 4.8 copy-start.3
  737.0 2.9 copy-start.4
  739.8 138.6 %all-gather.2.cloned.1.call-start = ((), (), s32[]{:S(2)}) async-start(), calls=%async_computation.3 | async-start | bytes 3899392 | tf_op jit(solution)/shard_map/all_gather | solution.py:41
Sparse Core Ops, SparseCore 0:
  10.4 84.9 reduce-scatter.1
  102.0 98.9 all-reduce.7
  217.4 59.8 all-reduce.9
  349.5 96.9 all-reduce.11
  455.1 86.2 all-reduce.13
  550.1 86.2 all-reduce.15
  645.0 86.2 all-reduce.17
  739.9 86.2 all-reduce.19
  828.4 50.0 all-gather.1
where the time goes:
time: 905 us; the launch traced here: 901 us
  waiting for transfers between devices  729 us (81%)
  matrix products  79.7 us (9%)
  blocking collectives  63.5 us (7%)
  between operations  15.6 us (2%)
    psum x5, waiting for transfers between devices, on_device(): gram_now = lax.psum(matmul(new_projector.T, new_projector), 'fsdp')  436 us
    psum x1, waiting for transfers between devices, on_device(): low_rank = lax.psum(matmul(projector.T, grad_total), 'fsdp')  98.8 us
    reduce_scatter x1, waiting for transfers between devices, on_device(): lax.psum_scatter(grad_parts[0].astype(jnp.float32).astype(jnp.bfloat16),...  87.5 us
    dot_general x19, matrix products, matmul(): jnp.dot(left, right, precision=lax.Precision.HIGHEST, preferred_element_t...  79.7 us
    psum x1, waiting for transfers between devices, on_device(): tangent = lax.psum(matmul(residual, low_rank.T), 'dp')  60 us
    all_gather x1, waiting for transfers between devices, on_device(): normed = lax.all_gather(normed_share, 'fsdp', axis=0, tiled=True)  45.6 us
    psum x1, blocking collectives, on_device(): tangent_sq = lax.psum(jnp.sum(tangent * tangent), 'fsdp')  34.1 us
    psum x1, blocking collectives, on_device(): frame_sq = lax.psum(jnp.sum(frame * frame), 'fsdp')  29.4 us
  transfers between devices with their start and end apart: 9, of which 9 were waited for; matrix products, arithmetic and copies ran while one was open for 1% of the time, Pallas kernels for 0%

commit v1 on v0

v1 whole, which is shorter than its diff:
```python
import jax
import jax.numpy as jnp
from jax import lax
from jax.experimental import pallas as pl
from jax.experimental.pallas import tpu as pltpu
from jax.sharding import PartitionSpec as P

NS_ITERS = 5

COEF_A = 3.4445
COEF_B = -4.775
COEF_C = 2.0315

MESH = pl.DeviceIdType.MESH
BF16 = jnp.bfloat16
F32 = jnp.float32

N_X = 4
N_DP = 8
N_FSDP = 16
CHUNK = 256
AHEAD = 3


def dot(left, right):
    return jnp.dot(left, right, preferred_element_type=F32)


def dot_nt(left, right):
    return lax.dot_general(left, right, (((1,), (1,)), ((), ())), preferred_element_type=F32)


def split(value):
    high = value.astype(BF16)
    return high, (value - high.astype(F32)).astype(BF16)


def dot3(left, right):
    return dot(left[0], right[0]) + dot(left[0], right[1]) + dot(left[1], right[0])


def diagonal(shape, row_at, col_at):
    rows = lax.broadcasted_iota(jnp.int32, shape, 0) + row_at
    cols = lax.broadcasted_iota(jnp.int32, shape, 1) + col_at
    return rows == cols


def fold_rows(value):
    rows, cols = value.shape
    part = jnp.sum(value.reshape(rows // 8, 8, cols), axis=0)
    total = part[:, 0:128]
    for at in range(128, cols, 128):
        total = total + part[:, at : at + 128]
    return total


def kernel(
    grad, weight, proj, avg, avg_sq,
    new_weight, new_proj, moment_one, moment_two,
    own, sib_in, opp_top, opp_bot, from_m, from_p,
    low_part, low_in, low_norm,
    w_buf, p_buf, m_buf, v_buf, p_bf, p_t, tan_acc,
    tan_send, tan_in, tan_all, gram_send, gram_in, gram_all,
    gram_buf, q_buf, out_buf,
    load_sem, own_sem, sib_ssem, sib_rsem, x_ssem, x_rsem,
    low_ssem, low_rsem, ln_ssem, ln_rsem, tail_ssem, tail_rsem, out_sem,
):
    rows = grad.shape[0]
    rank = proj.shape[1]
    share = avg.shape[0]
    owned = avg.shape[1]
    steps = owned // CHUNK
    half = rows // 2
    tan_rows = rank // N_DP

    d = lax.axis_index("dp")
    f = lax.axis_index("fsdp")
    x = d // 2
    core = d % 2
    sib = 2 * x + (1 - core)
    right = 2 * ((x + 1) % N_X) + core
    left = 2 * ((x + 3) % N_X) + core

    def remote(src, dst, ssem, rsem, device):
        return pltpu.make_async_remote_copy(
            src_ref=src, dst_ref=dst, send_sem=ssem, recv_sem=rsem, device_id=device, device_id_type=MESH
        )

    def columns(owner, j):
        return pl.ds(pl.multiple_of(owner * owned + j * CHUNK, CHUNK), CHUNK)

    def step_columns(j):
        return pl.ds(pl.multiple_of(j * CHUNK, CHUNK), CHUNK)

    def own_copy(q, j):
        return pltpu.make_async_copy(
            grad.at[:, columns(2 * ((x + q) % N_X) + core, j)], own.at[q, j], own_sem.at[j, q]
        )

    def sib_copy(q, j):
        return remote(
            grad.at[:, columns(2 * ((x + q) % N_X) + (1 - core), j)],
            sib_in.at[q, j], sib_ssem.at[j, q], sib_rsem.at[j, q], {"dp": sib},
        )

    top, bot = pl.ds(0, half), pl.ds(half, half)

    def x_copy(k, j):
        src, dst, device = (
            (lambda: (own.at[2, j, top], opp_top.at[j], right)),
            (lambda: (own.at[2, j, bot], opp_bot.at[j], left)),
            (lambda: (own.at[1, j, bot], from_m.at[j, bot], right)),
            (lambda: (own.at[3, j, top], from_p.at[j, top], left)),
            (lambda: (own.at[1, j, top], from_m.at[j, top], right)),
            (lambda: (own.at[3, j, bot], from_p.at[j, bot], left)),
        )[k]()
        return remote(src, dst, x_ssem.at[j, k], x_rsem.at[j, k], {"dp": device})

    loads = [
        pltpu.make_async_copy(proj, p_buf, load_sem.at[0]),
        pltpu.make_async_copy(avg, m_buf, load_sem.at[1]),
        pltpu.make_async_copy(avg_sq, v_buf, load_sem.at[2]),
        pltpu.make_async_copy(weight, w_buf, load_sem.at[3]),
    ]

    def start_loads(j):
        for q in (2, 1, 3, 0):
            own_copy(q, j).start()

    def start_sib(j):
        for q in (2, 1, 3, 0):
            sib_copy(q, j).start()

    start_loads(0)
    barrier = pltpu.get_barrier_semaphore()
    for i in range(1, N_DP):
        pl.semaphore_signal(barrier, inc=1, device_id={"dp": (d + i) % N_DP}, device_id_type=MESH)
    for i in range(1, N_FSDP):
        pl.semaphore_signal(barrier, inc=1, device_id={"fsdp": (f + i) % N_FSDP}, device_id_type=MESH)
    pl.semaphore_wait(barrier, N_DP + N_FSDP - 2)

    start_sib(0)
    for copy in loads:
        copy.start()
    for j in range(1, AHEAD):
        start_loads(j)
        start_sib(j)

    loads[0].wait()
    p_bf[...] = p_buf[...].astype(BF16)
    p_t[...] = dot_nt(diagonal((rank, rank), 0, 0).astype(BF16), p_bf[...]).astype(BF16)
    tan_acc[...] = jnp.zeros_like(tan_acc)
    for copy in loads[1:]:
        copy.wait()

    def pair_sum(q, j):
        own_copy(q, j).wait()
        sib_copy(q, j).wait_recv()
        return own[q, j].astype(F32) + sib_in[q, j].astype(F32)

    def stage_pair(j):
        own[2, j] = pair_sum(2, j).astype(BF16)
        x_copy(0, j).start()
        x_copy(1, j).start()
        own[1, j] = pair_sum(1, j).astype(BF16)
        x_copy(2, j).start()
        own[3, j] = pair_sum(3, j).astype(BF16)
        x_copy(3, j).start()

    def stage_pass(j):
        x_copy(0, j).wait_recv()
        own[1, j, top] = (own[1, j, top].astype(F32) + opp_top[j].astype(F32)).astype(BF16)
        x_copy(4, j).start()
        x_copy(1, j).wait_recv()
        own[3, j, bot] = (own[3, j, bot].astype(F32) + opp_bot[j].astype(F32)).astype(BF16)
        x_copy(5, j).start()

    def stage_low(j):
        total = pair_sum(0, j)
        for k in (2, 3, 4, 5):
            x_copy(k, j).wait_recv()
        total = (total + from_m[j].astype(F32) + from_p[j].astype(F32)).astype(BF16)
        own[0, j] = total
        low_part[j] = dot(p_t[...], total).astype(BF16).reshape(N_FSDP, share, CHUNK)

        @pl.loop(1, N_FSDP)
        def _(i):
            to = (f + i) % N_FSDP
            remote(low_part.at[j, to], low_in.at[j, f], low_ssem.at[j], low_rsem.at[j], {"fsdp": to}).start()

    def stage_adam(j):
        others = low_in.at[j, pl.ds(0, N_FSDP - 1)]
        low_in[j, f] = low_part[j, f]
        pltpu.make_async_copy(others, others, low_rsem.at[j]).wait()
        low = jnp.sum(low_in[j].astype(F32), axis=0)
        cols = step_columns(j)
        one = 0.9 * m_buf[:, cols] + 0.1 * low
        two = 0.999 * v_buf[:, cols] + 0.001 * low * low
        m_buf[:, cols] = one
        v_buf[:, cols] = two
        low_norm[j, f, 0] = low.astype(BF16)
        low_norm[j, f, 1] = (one / (jnp.sqrt(two) + 1e-08)).astype(BF16)

        @pl.loop(1, N_FSDP)
        def _(i):
            to = (f + i) % N_FSDP
            remote(low_norm.at[j, f], low_norm.at[j, f], ln_ssem.at[j], ln_rsem.at[j], {"fsdp": to}).start()

    def stage_tangent(j):
        others = low_norm.at[j, pl.ds(0, N_FSDP - 1)]
        pltpu.make_async_copy(others, others, ln_rsem.at[j]).wait()
        low = low_norm[j, :, 0].reshape(rank, CHUNK)
        resid = (own[0, j].astype(F32) - dot(p_bf[...], low)).astype(BF16)
        tan_acc[...] += dot_nt(resid, low)

    def stage_weight(j):
        cols = step_columns(j)
        update = dot(p_bf[...], low_norm[j, :, 1].reshape(rank, CHUNK))
        w_buf[:, cols] = (w_buf[:, cols].astype(F32) - 2.0 * update).astype(BF16)

    @pl.loop(0, steps + 4)
    def _(t):
        @pl.when(t + AHEAD < steps)
        def _():
            start_loads(t + AHEAD)
            start_sib(t + AHEAD)

        @pl.when(t < steps)
        def _():
            stage_pair(t)

        @pl.when((t >= 1) & (t < steps + 1))
        def _():
            stage_pass(t - 1)

        @pl.when((t >= 2) & (t < steps + 2))
        def _():
            stage_low(t - 2)

        @pl.when((t >= 3) & (t < steps + 3))
        def _():
            stage_adam(t - 3)

        @pl.when(t >= 4)
        def _():
            stage_tangent(t - 4)

    tan_send[...] = tan_acc[...].astype(BF16).reshape(N_DP, tan_rows, rank)

    @pl.loop(1, N_DP)
    def _(i):
        to = (d + i) % N_DP
        remote(tan_send.at[to], tan_in.at[d], tail_ssem.at[0], tail_rsem.at[0], {"dp": to}).start()

    tan_in[d] = tan_send[d]

    @pl.loop(0, steps)
    def _(j):
        stage_weight(j)

    outs = [
        pltpu.make_async_copy(w_buf, new_weight, out_sem.at[0]),
        pltpu.make_async_copy(m_buf, moment_one, out_sem.at[1]),
        pltpu.make_async_copy(v_buf, moment_two, out_sem.at[2]),
    ]
    for copy in outs:
        copy.start()

    others = tan_in.at[pl.ds(0, N_DP - 1)]
    pltpu.make_async_copy(others, others, tail_rsem.at[0]).wait()
    tan_all[d] = jnp.sum(tan_in[...].astype(F32), axis=0).astype(BF16)

    @pl.loop(1, N_DP)
    def _(i):
        to = (d + i) % N_DP
        remote(tan_all.at[d], tan_all.at[d], tail_ssem.at[1], tail_rsem.at[1], {"dp": to}).start()

    proj_sq = fold_rows(p_buf[...] * p_buf[...])
    pick = diagonal((tan_rows, rank), d * tan_rows, 0).astype(BF16)
    proj_pick = dot_nt(pick, p_bf[...]).astype(BF16)

    others = tan_all.at[pl.ds(0, N_DP - 1)]
    pltpu.make_async_copy(others, others, tail_rsem.at[1]).wait()

    tan = tan_all[...].reshape(rank, rank)
    tan_pick = dot_nt(pick, tan).astype(BF16)
    picks = jnp.concatenate([proj_pick, tan_pick], axis=0)
    with_proj = dot(picks, p_bf[...])
    with_tan = dot(picks, tan)
    gram_pp = with_proj[:tan_rows]
    gram_pt = with_proj[tan_rows:] + with_tan[:tan_rows]
    gram_tt = with_tan[tan_rows:]
    tan_f = tan.astype(F32)
    stats = jnp.concatenate([fold_rows(tan_f * tan_f), proj_sq], axis=0).astype(BF16)
    for to_y in range(4):
        for to_z in range(4):
            block = (slice(16 * to_y, 16 * to_y + 16), slice(128 * to_z, 128 * to_z + 128))
            at = 4 * to_y + to_z
            gram_send[at, 0:16] = gram_pp[block].astype(BF16)
            gram_send[at, 16:32] = gram_pt[block].astype(BF16)
            gram_send[at, 32:48] = gram_tt[block].astype(BF16)
            gram_send[at, 48:64] = stats

    @pl.loop(1, N_FSDP)
    def _(i):
        to = (f + i) % N_FSDP
        remote(gram_send.at[to], gram_in.at[f], tail_ssem.at[2], tail_rsem.at[2], {"fsdp": to}).start()

    gram_in[f] = gram_send[f]
    others = gram_in.at[pl.ds(0, N_FSDP - 1)]
    pltpu.make_async_copy(others, others, tail_rsem.at[2]).wait()
    sums = jnp.sum(gram_in[...].astype(F32), axis=0)
    tan_total = jnp.sum(sums[48:56])
    proj_total = jnp.sum(sums[56:64])
    tan_scale = 0.5 * jnp.sqrt(F32(rank)) / jnp.sqrt(jnp.full((1, 1), tan_total, F32) + 1e-06)
    middle = (proj_total + tan_scale * tan_scale * tan_total) / rank
    block = sums[0:16] + tan_scale * sums[16:32] + tan_scale * tan_scale * sums[32:48]
    on_diagonal = diagonal((16, 128), d * tan_rows + (f // 4) * 16, (f % 4) * 128)
    gram_all[d, f] = (block - jnp.where(on_diagonal, middle, 0.0)).astype(BF16)

    @pl.loop(1, N_FSDP)
    def _(i):
        to = (f + i) % N_FSDP
        remote(gram_all.at[d, f], gram_all.at[d, f], tail_ssem.at[3], tail_rsem.at[3], {"fsdp": to}).start()

    others = gram_all.at[d, pl.ds(0, N_FSDP - 1)]
    pltpu.make_async_copy(others, others, tail_rsem.at[3]).wait()

    @pl.loop(1, N_DP)
    def _(i):
        to = (d + i) % N_DP
        remote(gram_all.at[d], gram_all.at[d], tail_ssem.at[4], tail_rsem.at[4], {"dp": to}).start()

    frame = p_buf[...] + tan_scale * tan_f
    out_buf[...] = frame
    others = gram_all.at[pl.ds(0, N_DP - 1)]
    pltpu.make_async_copy(others, others, tail_rsem.at[4]).wait()

    eye = diagonal((rank, rank), 0, 0)
    whole = gram_all[...].astype(F32).reshape(N_DP, 4, 4, 16, 128)
    gram = jnp.concatenate([whole[:, :, at].reshape(rank, 128) for at in range(4)], axis=1)
    gram = gram + jnp.where(eye, middle, 0.0)
    frame_sq = jnp.sum(jnp.where(eye, gram, 0.0))
    frame_sq = jnp.full((1, 1), frame_sq, F32) + 1e-06
    gram_buf[...] = gram * (1.0 / frame_sq)
    q_buf[...] = jnp.where(eye, 1.0, 0.0)

    def polynomial(gram_parts):
        squared = dot3(gram_parts, gram_parts)
        return COEF_B * gram_buf[...] + COEF_C * squared + jnp.where(diagonal((rank, rank), 0, 0), COEF_A, 0.0)

    @pl.loop(0, NS_ITERS - 1)
    def _(sweep):
        gram_parts = split(gram_buf[...])
        poly = split(polynomial(gram_parts))
        once = dot3(gram_parts, poly)
        q_buf[...] = dot3(split(q_buf[...]), poly)
        gram_buf[...] = dot3(split(once), poly)

    poly = split(polynomial(split(gram_buf[...])))
    q_all = dot3(split(q_buf[...]), poly) * (1.0 / jnp.sqrt(frame_sq))
    out_buf[...] = dot3(split(out_buf[...]), split(q_all))
    last = pltpu.make_async_copy(out_buf, new_proj, out_sem.at[3])
    last.start()

    @pl.loop(0, steps)
    def _(j):
        for q in range(N_X):
            sib_copy(q, j).wait_send()
        for k in range(6):
            x_copy(k, j).wait_send()
        others = low_in.at[j, pl.ds(0, N_FSDP - 1)]
        pltpu.make_async_copy(others, others, low_ssem.at[j]).wait()
        others = low_norm.at[j, pl.ds(0, N_FSDP - 1)]
        pltpu.make_async_copy(others, others, ln_ssem.at[j]).wait()

    for k, others in enumerate(
        (
            tan_in.at[pl.ds(0, N_DP - 1)],
            tan_all.at[pl.ds(0, N_DP - 1)],
            gram_in.at[pl.ds(0, N_FSDP - 1)],
            gram_all.at[0, pl.ds(0, N_FSDP - 1)],
            gram_all.at[pl.ds(0, N_DP - 1)],
        )
    ):
        pltpu.make_async_copy(others, others, tail_ssem.at[k]).wait()
    for copy in outs:
        copy.wait()
    last.wait()


def on_device(grad_parts, weight, projector, exp_avg, exp_avg_sq):
    grad = grad_parts.reshape(grad_parts.shape[1:])
    rows = grad.shape[0]
    rank = projector.shape[1]
    share, owned = exp_avg.shape
    steps = owned // CHUNK
    tan_rows = rank // N_DP
    vmem = pltpu.VMEM
    dma = pltpu.SemaphoreType.DMA
    hbm = pl.BlockSpec(memory_space=pl.ANY)
    return pl.pallas_call(
        kernel,
        out_shape=(
            jax.ShapeDtypeStruct(weight.shape, weight.dtype),
            jax.ShapeDtypeStruct(projector.shape, projector.dtype),
            jax.ShapeDtypeStruct(exp_avg.shape, exp_avg.dtype),
            jax.ShapeDtypeStruct(exp_avg_sq.shape, exp_avg_sq.dtype),
        ),
        in_specs=[hbm] * 5,
        out_specs=(hbm,) * 4,
        scratch_shapes=[
            vmem((N_X, steps, rows, CHUNK), BF16),
            vmem((N_X, steps, rows, CHUNK), BF16),
            vmem((steps, rows // 2, CHUNK), BF16),
            vmem((steps, rows // 2, CHUNK), BF16),
            vmem((steps, rows, CHUNK), BF16),
            vmem((steps, rows, CHUNK), BF16),
            vmem((steps, N_FSDP, share, CHUNK), BF16),
            vmem((steps, N_FSDP, share, CHUNK), BF16),
            vmem((steps, N_FSDP, 2, share, CHUNK), BF16),
            vmem(weight.shape, BF16),
            vmem(projector.shape, F32),
            vmem(exp_avg.shape, F32),
            vmem(exp_avg_sq.shape, F32),
            vmem(projector.shape, BF16),
            vmem((rank, rows), BF16),
            vmem((rows, rank), F32),
            vmem((N_DP, tan_rows, rank), BF16),
            vmem((N_DP, tan_rows, rank), BF16),
            vmem((N_DP, tan_rows, rank), BF16),
            vmem((N_FSDP, 64, 128), BF16),
            vmem((N_FSDP, 64, 128), BF16),
            vmem((N_DP, N_FSDP, 16, 128), BF16),
            vmem((rank, rank), F32),
            vmem((rank, rank), F32),
            vmem((rows, rank), F32),
            dma((4,)),
            dma((steps, N_X)),
            dma((steps, N_X)),
            dma((steps, N_X)),
            dma((steps, 6)),
            dma((steps, 6)),
            dma((steps,)),
            dma((steps,)),
            dma((steps,)),
            dma((steps,)),
            dma((5,)),
            dma((5,)),
            dma((4,)),
        ],
        compiler_params=pltpu.CompilerParams(
            collective_id=0, has_side_effects=True, vmem_limit_bytes=60 * 1024 * 1024
        ),
    )(grad, weight, projector, exp_avg, exp_avg_sq)


def solution(mesh):
    return jax.shard_map(
        on_device,
        mesh=mesh,
        in_specs=(
            P("dp", "fsdp", None),
            P("fsdp", "dp"),
            P("fsdp", None),
            P("fsdp", "dp"),
            P("fsdp", "dp"),
        ),
        out_specs=(P("fsdp", "dp"), P("fsdp", None), P("fsdp", "dp"), P("fsdp", "dp")),
        check_vma=False,
    )
```

time: 905 us -> 159 us (0.18)
  waiting for transfers between devices: 729 us -> 0 us
  Pallas kernels: 0 us -> 153 us
  matrix products: 79.7 us -> 0 us
  blocking collectives: 63.5 us -> 0 us
  between operations: 15.6 us -> 0.65 us
    psum x7 -> x0, waiting for transfers between devices: 595 us -> none  [the longest x5 436 us: on_device(): gram_now = lax.psum(matmul(new_projector.T, new_projector), 'fsdp')]
    pallas_call x0 -> x1, Pallas kernels: none -> 153 us  [on_device(): pl.pallas_call(kernel, out_shape=(jax.ShapeDtypeStruct(weight.shape, weig...]
    reduce_scatter x1 -> x0, waiting for transfers between devices: 87.5 us -> none  [on_device(): lax.psum_scatter(grad_parts[0].astype(jnp.float32).astype(jnp.bfloat16),...]
    dot_general x19 -> x0, matrix products: 79.7 us -> none  [matmul(): jnp.dot(left, right, precision=lax.Precision.HIGHEST, preferred_element_t...]
    psum x2 -> x0, blocking collectives: 63.5 us -> none  [the longest x1 34.1 us: on_device(): tangent_sq = lax.psum(jnp.sum(tangent * tangent), 'fsdp')]
    all_gather x1 -> x0, waiting for transfers between devices: 45.6 us -> none  [on_device(): normed = lax.all_gather(normed_share, 'fsdp', axis=0, tiled=True)]
  transfers between devices with their start and end apart: 9 -> 0, of which waited for: 9 -> 0; matrix products, arithmetic and copies ran while one was open for 1% -> 0% of each run, Pallas kernels for 0% -> 0%
where the time goes in v1:
time: 159 us
  Pallas kernels  153 us (96%)
  local copies, waits for them, and re-layouts  5.47 us (3%)
    pallas_call x1, Pallas kernels, on_device(): pl.pallas_call(kernel, out_shape=(jax.ShapeDtypeStruct(weight.shape, weig...  153 us
    unnamed x10, local copies, waits for them, and re-layouts  5.47 us

profile of v1, /device:TPU:1, one launch (start us, length us, event | category | flops | bytes accessed | tf_op | source)
XLA Modules:
  0.0 158.9 jit_solution(7929312155802634052)
XLA Ops:
  0.6 152.7 %shard_map.84 = (bf16[512,1792]{1,0:T(8,128)(2,1)}, f32[512,512]{1,0:T(8,128)}, f32[32,1792]{1,0:T(8,128)}, f32[32,1792]{1,0:T(8,128)}) custom-call(bf16[512,14336]{1,0:T(8,128)(2,1)} %bitcast.1, bf16[512,1792]{1,0:T(8,128)(2,1)} %weight.1, f32[512,512]{1,0:T(8,128)} %proj.1, f32[32,1792]{1,0:T(8,128)} %avg.1, f32[32,1792]{1,0:T(8,128)} %avg_sq.1), custom_call_target="tpu_custom_call" | custom-call | tf_op jit(solution)/shard_map/pallas_call | solution.py:402
  153.4 0.0 copy-start
  153.4 2.9 %copy.13 = bf16[512,1792]{1,0:T(8,128)(2,1)} copy(bf16[512,1792]{1,0:T(8,128)(2,1)} %get-tuple-element.8) | data formatting | bytes 3670016
  156.3 0.0 copy-done
  156.3 0.0 copy-start.2
  156.3 0.0 copy-start.1
  156.3 1.0 copy.14
  157.3 0.2 copy-done.2
  157.5 0.7 copy.15
  158.2 0.0 copy-done.1
  158.2 0.7 copy.16
Async XLA Ops:
  153.4 2.9 %copy-start = (f32[512,512]{1,0:T(8,128)S(1)}, f32[512,512]{1,0:T(8,128)}, u32[]{:S(2)}) copy-start(f32[512,512]{1,0:T(8,128)} %get-tuple-element.9) | copy-start | bytes 3145732
  156.3 1.2 copy-start.2
  156.3 1.8 %copy-start.1 = (f32[32,1792]{1,0:T(8,128)S(1)}, f32[32,1792]{1,0:T(8,128)}, u32[]{:S(2)}) copy-start(f32[32,1792]{1,0:T(8,128)} %get-tuple-element.11) | copy-start | bytes 688132

commit v2 on v0

v2 whole, which is shorter than its diff:
```python
import jax
import jax.numpy as jnp
from jax import lax
from jax.experimental import pallas as pl
from jax.experimental.pallas import tpu as pltpu
from jax.sharding import PartitionSpec as P

NS_ITERS = 5

COEF_A = 3.4445
COEF_B = -4.775
COEF_C = 2.0315

MESH = pl.DeviceIdType.MESH
BF16 = jnp.bfloat16
F32 = jnp.float32

N_X = 4
N_DP = 8
N_FSDP = 16
N_CHIPS = N_X * N_FSDP
WIDTHS = (256,) * 7
AHEAD = 2
NORM_EARLY = 3


def dot(left, right):
    return jnp.dot(left, right, preferred_element_type=F32)


def dot_nt(left, right):
    return lax.dot_general(left, right, (((1,), (1,)), ((), ())), preferred_element_type=F32)


def diagonal(shape, row_at, col_at):
    rows = lax.broadcasted_iota(jnp.int32, shape, 0) + row_at
    cols = lax.broadcasted_iota(jnp.int32, shape, 1) + col_at
    return rows == cols


def fold_rows(value):
    rows, cols = value.shape
    part = jnp.sum(value.reshape(rows // 8, 8, cols), axis=0)
    total = part[:, 0:128]
    for at in range(128, cols, 128):
        total = total + part[:, at : at + 128]
    return total


def kernel(
    grad, weight, proj, avg, avg_sq,
    new_weight, moment_one, moment_two, tan_out, gram_out, scale_out,
    own, sib_in, opp_top, opp_bot, from_m, from_p,
    low_part, low_in, low_all, norm_all,
    w_buf, p_buf, m_buf, v_buf, p_bf, p_t, tan_acc,
    tan_send, tan_sib, tan_x, tan_in, tan_all, gram_send, gram_in, gram_all, scale_buf,
    load_sem, own_sem, sib_ssem, sib_rsem, x_ssem, x_rsem,
    low_ssem, low_rsem, all_ssem, all_rsem, norm_ssem, norm_rsem, tail_ssem, tail_rsem, out_sem,
):
    rows = grad.shape[0]
    rank = proj.shape[1]
    owned = avg.shape[1]
    steps = len(WIDTHS)
    half = rows // 2
    tan_rows = rank // N_DP

    d = lax.axis_index("dp")
    f = lax.axis_index("fsdp")
    x = d // 2
    core = d % 2
    sib = {"dp": 2 * x + (1 - core)}
    right = {"dp": 2 * ((x + 1) % N_X) + core}
    left = {"dp": 2 * ((x + 3) % N_X) + core}

    def remote(src, dst, ssem, rsem, device):
        return pltpu.make_async_remote_copy(
            src_ref=src, dst_ref=dst, send_sem=ssem, recv_sem=rsem, device_id=device, device_id_type=MESH
        )

    def wait_bytes(ref, sem):
        pltpu.make_async_copy(ref, ref, sem).wait()

    def to_fsdp(src_of, dst, ssem, rsem):
        @pl.loop(1, N_FSDP)
        def _(i):
            to = (f + i) % N_FSDP
            remote(src_of(to), dst, ssem, rsem, {"fsdp": to}).start()

    def to_x(src_of, dst, ssem, rsem):
        for i in (2, 1, 3):
            to = (x + i) % N_X
            remote(src_of(to), dst, ssem, rsem, {"dp": 2 * to + core}).start()

    def chip_at(i):
        to = (x * N_FSDP + f + i) % N_CHIPS
        return {"dp": 2 * (to // N_FSDP) + core, "fsdp": to % N_FSDP}

    starts = [sum(WIDTHS[:j]) for j in range(steps)]
    cols = [pl.ds(starts[j], WIDTHS[j]) for j in range(steps)]

    def columns(owner, j):
        return pl.ds(pl.multiple_of(owner * owned + starts[j], 128), WIDTHS[j])

    def own_copy(q, j):
        return pltpu.make_async_copy(
            grad.at[:, columns(2 * ((x + q) % N_X) + core, j)], own.at[q, :, cols[j]], own_sem.at[j, q]
        )

    def sib_copy(q, j):
        return remote(
            grad.at[:, columns(2 * ((x + q) % N_X) + (1 - core), j)],
            sib_in.at[q, :, cols[j]], sib_ssem.at[j, q], sib_rsem.at[j, q], sib,
        )

    top, bot = pl.ds(0, half), pl.ds(half, half)

    def x_copy(k, j):
        c = cols[j]
        src, dst, device = (
            (own.at[2, top, c], opp_top.at[:, c], right),
            (own.at[2, bot, c], opp_bot.at[:, c], left),
            (own.at[1, bot, c], from_m.at[bot, c], right),
            (own.at[3, top, c], from_p.at[top, c], left),
            (own.at[1, top, c], from_m.at[top, c], right),
            (own.at[3, bot, c], from_p.at[bot, c], left),
        )[k]
        return remote(src, dst, x_ssem.at[j, k], x_rsem.at[j, k], device)

    loads = [
        pltpu.make_async_copy(proj, p_buf, load_sem.at[0]),
        pltpu.make_async_copy(avg, m_buf, load_sem.at[1]),
        pltpu.make_async_copy(avg_sq, v_buf, load_sem.at[2]),
        pltpu.make_async_copy(weight, w_buf, load_sem.at[3]),
    ]

    def start_loads(j):
        for q in (2, 1, 3, 0):
            own_copy(q, j).start()

    def start_sib(j):
        for q in (2, 1, 3, 0):
            sib_copy(q, j).start()

    loads[0].start()
    start_loads(0)
    barrier = pltpu.get_barrier_semaphore()
    pl.semaphore_signal(barrier, inc=1, device_id=sib, device_id_type=MESH)
    for i in range(1, N_CHIPS):
        pl.semaphore_signal(barrier, inc=1, device_id=chip_at(i), device_id_type=MESH)
    loads[0].wait()
    p_bf[...] = p_buf[...].astype(BF16)
    p_t[...] = dot_nt(diagonal((rank, rank), 0, 0).astype(BF16), p_bf[...]).astype(BF16)
    pl.semaphore_wait(barrier, N_CHIPS)

    def pair_sum(q, j):
        own_copy(q, j).wait()
        sib_copy(q, j).wait_recv()
        return own[q, :, cols[j]].astype(F32) + sib_in[q, :, cols[j]].astype(F32)

    def stage_pair(j):
        own[2, :, cols[j]] = pair_sum(2, j).astype(BF16)
        x_copy(0, j).start()
        x_copy(1, j).start()
        own[1, :, cols[j]] = pair_sum(1, j).astype(BF16)
        x_copy(2, j).start()
        own[3, :, cols[j]] = pair_sum(3, j).astype(BF16)
        x_copy(3, j).start()

    def stage_pass(j):
        c = cols[j]
        x_copy(0, j).wait_recv()
        own[1, top, c] = (own[1, top, c].astype(F32) + opp_top[:, c].astype(F32)).astype(BF16)
        x_copy(4, j).start()
        x_copy(1, j).wait_recv()
        own[3, bot, c] = (own[3, bot, c].astype(F32) + opp_bot[:, c].astype(F32)).astype(BF16)
        x_copy(5, j).start()

    def stage_low(j):
        c = cols[j]
        total = pair_sum(0, j)
        for k in (2, 3, 4, 5):
            x_copy(k, j).wait_recv()
        total = (total + from_m[:, c].astype(F32) + from_p[:, c].astype(F32)).astype(BF16)
        own[0, :, c] = total
        low_part[:, :, c] = dot(p_t[...], total).astype(BF16).reshape(N_FSDP, -1, WIDTHS[j])
        to_fsdp(lambda to: low_part.at[to, :, c], low_in.at[f, :, c], low_ssem.at[j], low_rsem.at[j])

    def stage_adam(j):
        c = cols[j]
        low_in[f, :, c] = low_part[f, :, c]
        wait_bytes(low_in.at[pl.ds(0, N_FSDP - 1), :, c], low_rsem.at[j])
        low = jnp.sum(low_in[:, :, c].astype(F32), axis=0)
        low_all[f, :, c] = low.astype(BF16)
        to_fsdp(lambda to: low_all.at[f, :, c], low_all.at[f, :, c], all_ssem.at[j], all_rsem.at[j])
        one = 0.9 * m_buf[:, c] + 0.1 * low
        two = 0.999 * v_buf[:, c] + 0.001 * low * low
        m_buf[:, c] = one
        v_buf[:, c] = two
        norm_all[f, :, c] = (one / (jnp.sqrt(two) + 1e-08)).astype(BF16)

    def stage_norm(j):
        c = cols[j]
        to_fsdp(lambda to: norm_all.at[f, :, c], norm_all.at[f, :, c], norm_ssem.at[j], norm_rsem.at[j])

    def stage_tangent(j):
        c = cols[j]
        wait_bytes(low_all.at[pl.ds(0, N_FSDP - 1), :, c], all_rsem.at[j])
        low = low_all[:, :, c].reshape(rank, WIDTHS[j])
        resid = (own[0, :, c].astype(F32) - dot(p_bf[...], low)).astype(BF16)
        if j == 0:
            tan_acc[...] = dot_nt(resid, low)
        else:
            tan_acc[...] += dot_nt(resid, low)

    def weight_copy(j):
        return pltpu.make_async_copy(w_buf.at[:, cols[j]], new_weight.at[:, cols[j]], out_sem.at[j])

    def stage_weight(j):
        c = cols[j]
        wait_bytes(norm_all.at[pl.ds(0, N_FSDP - 1), :, c], norm_rsem.at[j])
        update = dot(p_bf[...], norm_all[:, :, c].reshape(rank, WIDTHS[j]))
        w_buf[:, c] = (w_buf[:, c].astype(F32) - 2.0 * update).astype(BF16)
        weight_copy(j).start()

    start_sib(0)
    for j in range(1, AHEAD):
        start_loads(j)
        start_sib(j)
    for copy in loads[1:]:
        copy.start()

    for t in range(steps + 4):
        if t + AHEAD < steps:
            start_loads(t + AHEAD)
            start_sib(t + AHEAD)
        if t < steps:
            stage_pair(t)
        if t == 1:
            for copy in loads[1:]:
                copy.wait()
        if 1 <= t < steps + 1:
            stage_pass(t - 1)
        if 2 <= t < steps + 2:
            stage_low(t - 2)
        if 3 <= t < steps + 3:
            stage_adam(t - 3)
        if 4 <= t:
            stage_tangent(t - 4)
            if t - 4 < NORM_EARLY:
                stage_norm(t - 4)
        if 6 <= t < NORM_EARLY + 6:
            stage_weight(t - 6)

    tan_send[...] = tan_acc[...].astype(BF16).reshape(N_X, 2, tan_rows, rank)
    pair_copy = remote(tan_send.at[:, 1 - core], tan_sib, tail_ssem.at[0], tail_rsem.at[0], sib)
    pair_copy.start()
    pair_copy.wait_recv()
    tan_x[...] = (tan_send[:, core].astype(F32) + tan_sib[...].astype(F32)).astype(BF16)
    to_x(lambda to: tan_x.at[to], tan_in.at[x], tail_ssem.at[1], tail_rsem.at[1])
    tan_in[x] = tan_x[x]
    for j in range(NORM_EARLY, steps):
        stage_norm(j)
    outs = [
        pltpu.make_async_copy(m_buf, moment_one, out_sem.at[steps]),
        pltpu.make_async_copy(v_buf, moment_two, out_sem.at[steps + 1]),
    ]
    for copy in outs:
        copy.start()
    wait_bytes(tan_in.at[pl.ds(0, N_X - 1)], tail_rsem.at[1])
    tan_all[x, core] = jnp.sum(tan_in[...].astype(F32), axis=0).astype(BF16)
    to_x(lambda to: tan_all.at[x, core], tan_all.at[x, core], tail_ssem.at[2], tail_rsem.at[2])

    for j in range(NORM_EARLY, NORM_EARLY + 2):
        stage_weight(j)
    proj_sq = fold_rows(p_buf[...] * p_buf[...])
    pick = diagonal((tan_rows, rank), d * tan_rows, 0).astype(BF16)
    proj_pick = dot_nt(pick, p_bf[...]).astype(BF16)

    wait_bytes(tan_all.at[pl.ds(0, N_X - 1), 0], tail_rsem.at[2])
    pair_all = remote(tan_all.at[:, core], tan_all.at[:, core], tail_ssem.at[3], tail_rsem.at[3], sib)
    pair_all.start()
    pair_all.wait_recv()

    tan = tan_all[...].reshape(rank, rank)
    tan_copy = pltpu.make_async_copy(tan_all, tan_out, out_sem.at[steps + 2])
    tan_copy.start()
    tan_pick = dot_nt(pick, tan).astype(BF16)
    picks = jnp.concatenate([proj_pick, tan_pick], axis=0)
    with_proj = dot(picks, p_bf[...])
    with_tan = dot(picks, tan)
    gram_pp = with_proj[:tan_rows]
    gram_pt = with_proj[tan_rows:] + with_tan[:tan_rows]
    gram_tt = with_tan[tan_rows:]
    tan_f = tan.astype(F32)
    stats = jnp.concatenate([fold_rows(tan_f * tan_f), proj_sq], axis=0).astype(BF16)
    for to_y in range(4):
        for to_z in range(4):
            block = (slice(16 * to_y, 16 * to_y + 16), slice(128 * to_z, 128 * to_z + 128))
            at = 4 * to_y + to_z
            gram_send[at, 0:16] = gram_pp[block].astype(BF16)
            gram_send[at, 16:32] = gram_pt[block].astype(BF16)
            gram_send[at, 32:48] = gram_tt[block].astype(BF16)
            gram_send[at, 48:64] = stats
    to_fsdp(lambda to: gram_send.at[to], gram_in.at[f], tail_ssem.at[4], tail_rsem.at[4])
    gram_in[f] = gram_send[f]
    for j in range(NORM_EARLY + 2, steps):
        stage_weight(j)
    wait_bytes(gram_in.at[pl.ds(0, N_FSDP - 1)], tail_rsem.at[4])
    sums = jnp.sum(gram_in[...].astype(F32), axis=0)
    tan_total = jnp.sum(sums[48:56])
    proj_total = jnp.sum(sums[56:64])
    tan_scale = 0.5 * jnp.sqrt(F32(rank)) / jnp.sqrt(jnp.full((1, 1), tan_total, F32) + 1e-06)
    middle = (proj_total + tan_scale * tan_scale * tan_total) / rank
    block = sums[0:16] + tan_scale * sums[16:32] + tan_scale * tan_scale * sums[32:48]
    on_diagonal = diagonal((16, 128), d * tan_rows + (f // 4) * 16, (f % 4) * 128)
    gram_all[x, core, f] = (block - jnp.where(on_diagonal, middle, 0.0)).astype(BF16)
    mine = gram_all.at[x, core, f]

    @pl.loop(1, N_CHIPS)
    def _(i):
        remote(mine, mine, tail_ssem.at[5], tail_rsem.at[5], chip_at(i)).start()

    scale_buf[0:8] = jnp.broadcast_to(tan_scale, (8, 128))
    scale_buf[8:16] = jnp.broadcast_to(middle, (8, 128))
    scale_copy = pltpu.make_async_copy(scale_buf, scale_out, out_sem.at[steps + 3])
    scale_copy.start()
    blocks = own.at[0, pl.ds(0, 144), pl.ds(0, 896)]
    wait_bytes(blocks, tail_rsem.at[5])
    pair_gram = remote(gram_all.at[:, core], gram_all.at[:, core], tail_ssem.at[7], tail_rsem.at[7], sib)
    pair_gram.start()
    pair_gram.wait_recv()
    gram_copy = pltpu.make_async_copy(gram_all, gram_out, out_sem.at[steps + 4])
    gram_copy.start()

    for j in range(steps):
        c = cols[j]
        for q in range(N_X):
            sib_copy(q, j).wait_send()
        for k in range(6):
            x_copy(k, j).wait_send()
        wait_bytes(low_in.at[pl.ds(0, N_FSDP - 1), :, c], low_ssem.at[j])
        wait_bytes(low_all.at[pl.ds(0, N_FSDP - 1), :, c], all_ssem.at[j])
        wait_bytes(norm_all.at[pl.ds(0, N_FSDP - 1), :, c], norm_ssem.at[j])
        weight_copy(j).wait()
    pair_copy.wait_send()
    wait_bytes(tan_in.at[pl.ds(0, N_X - 1)], tail_ssem.at[1])
    wait_bytes(tan_all.at[pl.ds(0, N_X - 1), 0], tail_ssem.at[2])
    pair_all.wait_send()
    wait_bytes(gram_in.at[pl.ds(0, N_FSDP - 1)], tail_ssem.at[4])
    wait_bytes(blocks, tail_ssem.at[5])
    pair_gram.wait_send()
    for copy in outs:
        copy.wait()
    tan_copy.wait()
    scale_copy.wait()
    gram_copy.wait()


def finish_kernel(
    weight_in, one_in, two_in, tan, gram, scale, proj,
    new_weight, new_proj, moment_one, moment_two,
    tan_buf, gram_buf, scale_buf, proj_buf, w_state, q_state, out_buf, weight_buf, one_buf, two_buf, sems,
):
    rank = proj.shape[1]
    copies = [
        pltpu.make_async_copy(gram, gram_buf, sems.at[0]),
        pltpu.make_async_copy(scale, scale_buf, sems.at[1]),
        pltpu.make_async_copy(tan, tan_buf, sems.at[2]),
        pltpu.make_async_copy(proj, proj_buf, sems.at[3]),
        pltpu.make_async_copy(weight_in, weight_buf, sems.at[4]),
        pltpu.make_async_copy(one_in, one_buf, sems.at[5]),
        pltpu.make_async_copy(two_in, two_buf, sems.at[6]),
    ]
    passed = [
        pltpu.make_async_copy(weight_buf, new_weight, sems.at[4]),
        pltpu.make_async_copy(one_buf, moment_one, sems.at[5]),
        pltpu.make_async_copy(two_buf, moment_two, sems.at[6]),
    ]
    for copy in copies:
        copy.start()
    copies[0].wait()
    copies[1].wait()
    tan_scale = scale_buf[0:1, 0:1]
    middle = scale_buf[8:9, 0:1]
    eye = diagonal((rank, rank), 0, 0)
    whole = gram_buf[...].astype(F32).reshape(N_DP, 4, 4, 16, 128)
    gram_dev = jnp.concatenate([whole[:, :, at].reshape(rank, 128) for at in range(4)], axis=1)
    trace_dev = jnp.sum(jnp.sum(jnp.where(eye, gram_dev, 0.0), axis=0, keepdims=True), axis=1, keepdims=True)
    frame_sq = trace_dev + rank * middle + 1e-06
    inverse = 1.0 / frame_sq
    shift = trace_dev / rank
    center = (middle + shift) * inverse
    state = (gram_dev - jnp.where(eye, shift, 0.0)) * inverse
    w_state[...] = state
    q_center = None
    for sweep in range(NS_ITERS):
        state = w_state[...]
        state_b = state.astype(BF16)
        poly = (COEF_B + 2.0 * COEF_C * center) * state + COEF_C * dot(state_b, state_b)
        poly_center = COEF_A + COEF_B * center + COEF_C * center * center
        poly_b = poly.astype(BF16)
        if sweep == 0:
            q_state[...] = poly
            q_center = poly_center
        else:
            q_now = q_state[...]
            q_state[...] = q_center * poly + poly_center * q_now + dot(q_now.astype(BF16), poly_b)
            q_center = q_center * poly_center
        if sweep == 0:
            for copy, on in zip(copies[4:], passed):
                copy.wait()
                on.start()
        if sweep < NS_ITERS - 1:
            once = center * poly + poly_center * state + dot(state_b, poly_b)
            once_center = center * poly_center
            w_state[...] = once_center * poly + poly_center * once + dot(once.astype(BF16), poly_b)
            center = once_center * poly_center
    q_now = q_state[...]
    q_shift = jnp.sum(jnp.sum(jnp.where(eye, q_now, 0.0), axis=0, keepdims=True), axis=1, keepdims=True) / rank
    q_b = (q_now - jnp.where(eye, q_shift, 0.0)).astype(BF16)
    copies[2].wait()
    copies[3].wait()
    scale_down = 1.0 / jnp.sqrt(frame_sq)
    frame = (proj_buf[...] + tan_scale * tan_buf[...].reshape(rank, rank).astype(F32)) * scale_down
    out_buf[...] = (q_center + q_shift) * frame + dot(frame.astype(BF16), q_b)
    last = pltpu.make_async_copy(out_buf, new_proj, sems.at[7])
    last.start()
    for copy in passed:
        copy.wait()
    last.wait()


def on_device(grad_parts, weight, projector, exp_avg, exp_avg_sq):
    grad = grad_parts.reshape(grad_parts.shape[1:])
    rows = grad.shape[0]
    rank = projector.shape[1]
    share, owned = exp_avg.shape
    steps = len(WIDTHS)
    tan_rows = rank // N_DP
    vmem = pltpu.VMEM
    dma = pltpu.SemaphoreType.DMA
    hbm = pl.BlockSpec(memory_space=pl.ANY)
    shape = jax.ShapeDtypeStruct
    tan_shape = (N_X, 2, tan_rows, rank)
    gram_shape = (N_X, 2, N_FSDP, 16, 128)
    mid = pl.pallas_call(
        kernel,
        out_shape=(
            shape(weight.shape, weight.dtype),
            shape(exp_avg.shape, F32),
            shape(exp_avg_sq.shape, F32),
            shape(tan_shape, BF16),
            shape(gram_shape, BF16),
            shape((16, 128), F32),
        ),
        in_specs=[hbm] * 5,
        out_specs=(hbm,) * 6,
        scratch_shapes=[
            vmem((N_X, rows, owned), BF16),
            vmem((N_X, rows, owned), BF16),
            vmem((rows // 2, owned), BF16),
            vmem((rows // 2, owned), BF16),
            vmem((rows, owned), BF16),
            vmem((rows, owned), BF16),
            vmem((N_FSDP, share, owned), BF16),
            vmem((N_FSDP, share, owned), BF16),
            vmem((N_FSDP, share, owned), BF16),
            vmem((N_FSDP, share, owned), BF16),
            vmem(weight.shape, BF16),
            vmem(projector.shape, F32),
            vmem(exp_avg.shape, F32),
            vmem(exp_avg_sq.shape, F32),
            vmem(projector.shape, BF16),
            vmem((rank, rows), BF16),
            vmem((rows, rank), F32),
            vmem(tan_shape, BF16),
            vmem((N_X, tan_rows, rank), BF16),
            vmem((N_X, tan_rows, rank), BF16),
            vmem((N_X, tan_rows, rank), BF16),
            vmem(tan_shape, BF16),
            vmem((N_FSDP, 64, 128), BF16),
            vmem((N_FSDP, 64, 128), BF16),
            vmem(gram_shape, BF16),
            vmem((16, 128), F32),
            dma((4,)),
            dma((steps, N_X)),
            dma((steps, N_X)),
            dma((steps, N_X)),
            dma((steps, 6)),
            dma((steps, 6)),
            dma((steps,)),
            dma((steps,)),
            dma((steps,)),
            dma((steps,)),
            dma((steps,)),
            dma((steps,)),
            dma((8,)),
            dma((8,)),
            dma((steps + 5,)),
        ],
        compiler_params=pltpu.CompilerParams(
            collective_id=0, has_side_effects=True, vmem_limit_bytes=60 * 1024 * 1024
        ),
    )(grad, weight, projector, exp_avg, exp_avg_sq)
    return pl.pallas_call(
        finish_kernel,
        out_shape=(
            shape(weight.shape, weight.dtype),
            shape(projector.shape, F32),
            shape(exp_avg.shape, F32),
            shape(exp_avg_sq.shape, F32),
        ),
        in_specs=[hbm] * 7,
        out_specs=(hbm,) * 4,
        scratch_shapes=[
            vmem(tan_shape, BF16),
            vmem(gram_shape, BF16),
            vmem((16, 128), F32),
            vmem(projector.shape, F32),
            vmem((rank, rank), F32),
            vmem((rank, rank), F32),
            vmem(projector.shape, F32),
            vmem(weight.shape, BF16),
            vmem(exp_avg.shape, F32),
            vmem(exp_avg_sq.shape, F32),
            dma((8,)),
        ],
        compiler_params=pltpu.CompilerParams(vmem_limit_bytes=60 * 1024 * 1024),
    )(*mid, projector)


def solution(mesh):
    return jax.shard_map(
        on_device,
        mesh=mesh,
        in_specs=(
            P("dp", "fsdp", None),
            P("fsdp", "dp"),
            P("fsdp", None),
            P("fsdp", "dp"),
            P("fsdp", "dp"),
        ),
        out_specs=(P("fsdp", "dp"), P("fsdp", None), P("fsdp", "dp"), P("fsdp", "dp")),
        check_vma=False,
    )
```

time: 905 us -> 133 us (0.15)
  waiting for transfers between devices: 729 us -> 0 us
  Pallas kernels: 0 us -> 132 us
  matrix products: 79.7 us -> 0 us
  blocking collectives: 63.5 us -> 0 us
  between operations: 15.6 us -> 0.8 us
    psum x7 -> x0, waiting for transfers between devices: 595 us -> none  [the longest x5 436 us: on_device(): gram_now = lax.psum(matmul(new_projector.T, new_projector), 'fsdp')]
    pallas_call x0 -> x2, Pallas kernels: none -> 132 us  [the longest x1 123 us: on_device(): pl.pallas_call(kernel, out_shape=(shape(weight.shape, weight.dtype), shap...]
    reduce_scatter x1 -> x0, waiting for transfers between devices: 87.5 us -> none  [on_device(): lax.psum_scatter(grad_parts[0].astype(jnp.float32).astype(jnp.bfloat16),...]
    dot_general x19 -> x0, matrix products: 79.7 us -> none  [matmul(): jnp.dot(left, right, precision=lax.Precision.HIGHEST, preferred_element_t...]
    psum x2 -> x0, blocking collectives: 63.5 us -> none  [the longest x1 34.1 us: on_device(): tangent_sq = lax.psum(jnp.sum(tangent * tangent), 'fsdp')]
    all_gather x1 -> x0, waiting for transfers between devices: 45.6 us -> none  [on_device(): normed = lax.all_gather(normed_share, 'fsdp', axis=0, tiled=True)]
  transfers between devices with their start and end apart: 9 -> 0, of which waited for: 9 -> 0; matrix products, arithmetic and copies ran while one was open for 1% -> 0% of each run, Pallas kernels for 0% -> 0%
where the time goes in v2:
time: 133 us
  Pallas kernels  132 us (99%)
    pallas_call x1, Pallas kernels, on_device(): pl.pallas_call(kernel, out_shape=(shape(weight.shape, weight.dtype), shap...  123 us
    pallas_call x1, Pallas kernels, on_device(): pl.pallas_call(finish_kernel, out_shape=(shape(weight.shape, weight.dtype...  9.26 us

profile of v2, /device:TPU:1, one launch (start us, length us, event | category | flops | bytes accessed | tf_op | source)
XLA Modules:
  0.0 132.8 jit_solution(1051288238300466635)
XLA Ops:
  0.6 122.7 %shard_map.84 = (bf16[512,1792]{1,0:T(8,128)(2,1)}, f32[32,1792]{1,0:T(8,128)}, f32[32,1792]{1,0:T(8,128)}, bf16[4,2,64,512]{3,2,1,0:T(8,128)(2,1)}, bf16[4,2,16...) custom-call(bf16[512,14336]{1,0:T(8,128)(2,1)} %bitcast.1, bf16[512,1792]{1,0:T(8,128)(2,1)} %weight.1, f32[512,512]{1,0:T(8,128)} %proj.3, ...), custom_call_target="tpu_custom_call" | custom-call | tf_op jit(solution)/shard_map/pallas_call | solution.py:446
  123.3 9.3 %shard_map.85 = (bf16[512,1792]{1,0:T(8,128)(2,1)}, f32[512,512]{1,0:T(8,128)}, f32[32,1792]{1,0:T(8,128)}, f32[32,1792]{1,0:T(8,128)}) custom-call(bf16[512,1792]{1,0:T(8,128)(2,1)} %get-tuple-element.10.weight_in, f32[32,1792]{1,0:T(8,128)} %get-tuple-element.11.one_in, f32[32,1792]{1,0:T(8,128)} %get-tuple-element.12.two_in, ...), custom_call_target="tpu_custom_call" | custom-call | tf_op jit(solution)/shard_map/pallas_call | solution.py:505

commit v3 on v2

--- a/solution.py
+++ b/solution.py
@@ -66,11 +66,16 @@
 
     d = lax.axis_index("dp")
     f = lax.axis_index("fsdp")
-    x = d // 2
-    core = d % 2
+    x, core = lax.div(d, 2), lax.rem(d, 2)
+    y, z = lax.div(f, 4), lax.rem(f, 4)
+    xs = [lax.rem(x + i, N_X) for i in range(N_X)]
+    ys = [lax.rem(y + i, 4) for i in range(4)]
+    zs = [lax.rem(z + i, 4) for i in range(4)]
+    far = (2, 1, 3, 0)
+    hops = (0, 1, 2, 1)
     sib = {"dp": 2 * x + (1 - core)}
-    right = {"dp": 2 * ((x + 1) % N_X) + core}
-    left = {"dp": 2 * ((x + 3) % N_X) + core}
+    right = {"dp": 2 * xs[1] + core}
+    left = {"dp": 2 * xs[3] + core}
 
     def remote(src, dst, ssem, rsem, device):
         return pltpu.make_async_remote_copy(
@@ -80,20 +85,31 @@
     def wait_bytes(ref, sem):
         pltpu.make_async_copy(ref, ref, sem).wait()
 
-    def to_fsdp(src_of, dst, ssem, rsem):
+    planes = sorted(((i, j) for i in range(4) for j in range(4)), key=lambda at: -hops[at[0]] - hops[at[1]])[:-1]
+    chips = sorted(
+        ((k, i, j) for k in range(4) for i in range(4) for j in range(4)),
+        key=lambda at: -hops[at[0]] - hops[at[1]] - hops[at[2]],
+    )[:-1]
+
+    def to_fsdp(src_of, dst, ssem, rsem, ordered=False):
+        if ordered:
+            for i, j in planes:
+                to = 4 * ys[i] + zs[j]
+                remote(src_of(to), dst, ssem, rsem, {"fsdp": to}).start()
+            return
+
         @pl.loop(1, N_FSDP)
         def _(i):
-            to = (f + i) % N_FSDP
+            to = lax.rem(f + i, N_FSDP)
             remote(src_of(to), dst, ssem, rsem, {"fsdp": to}).start()
 
     def to_x(src_of, dst, ssem, rsem):
-        for i in (2, 1, 3):
-            to = (x + i) % N_X
+        for i in far[:3]:
+            to = xs[i]
             remote(src_of(to), dst, ssem, rsem, {"dp": 2 * to + core}).start()
 
-    def chip_at(i):
-        to = (x * N_FSDP + f + i) % N_CHIPS
-        return {"dp": 2 * (to // N_FSDP) + core, "fsdp": to % N_FSDP}
+    def chip_at(at):
+        return {"dp": 2 * xs[at[0]] + core, "fsdp": 4 * ys[at[1]] + zs[at[2]]}
 
     starts = [sum(WIDTHS[:j]) for j in range(steps)]
     cols = [pl.ds(starts[j], WIDTHS[j]) for j in range(steps)]
@@ -103,12 +119,12 @@
 
     def own_copy(q, j):
         return pltpu.make_async_copy(
-            grad.at[:, columns(2 * ((x + q) % N_X) + core, j)], own.at[q, :, cols[j]], own_sem.at[j, q]
+            grad.at[:, columns(2 * xs[q] + core, j)], own.at[q, :, cols[j]], own_sem.at[j, q]
         )
 
     def sib_copy(q, j):
         return remote(
-            grad.at[:, columns(2 * ((x + q) % N_X) + (1 - core), j)],
+            grad.at[:, columns(2 * xs[q] + (1 - core), j)],
             sib_in.at[q, :, cols[j]], sib_ssem.at[j, q], sib_rsem.at[j, q], sib,
         )
 
@@ -146,10 +162,9 @@
     barrier = pltpu.get_barrier_semaphore()
     pl.semaphore_signal(barrier, inc=1, device_id=sib, device_id_type=MESH)
     for i in range(1, N_CHIPS):
-        pl.semaphore_signal(barrier, inc=1, device_id=chip_at(i), device_id_type=MESH)
-    loads[0].wait()
-    p_bf[...] = p_buf[...].astype(BF16)
-    p_t[...] = dot_nt(diagonal((rank, rank), 0, 0).astype(BF16), p_bf[...]).astype(BF16)
+        to = lax.rem(x * N_FSDP + f + i, N_CHIPS)
+        device = {"dp": 2 * lax.div(to, N_FSDP) + core, "fsdp": lax.rem(to, N_FSDP)}
+        pl.semaphore_signal(barrier, inc=1, device_id=device, device_id_type=MESH)
     pl.semaphore_wait(barrier, N_CHIPS)
 
     def pair_sum(q, j):
@@ -157,10 +172,12 @@
         sib_copy(q, j).wait_recv()
         return own[q, :, cols[j]].astype(F32) + sib_in[q, :, cols[j]].astype(F32)
 
-    def stage_pair(j):
+    def stage_opposite(j):
         own[2, :, cols[j]] = pair_sum(2, j).astype(BF16)
         x_copy(0, j).start()
         x_copy(1, j).start()
+
+    def stage_pair(j):
         own[1, :, cols[j]] = pair_sum(1, j).astype(BF16)
         x_copy(2, j).start()
         own[3, :, cols[j]] = pair_sum(3, j).astype(BF16)
@@ -183,7 +200,7 @@
         total = (total + from_m[:, c].astype(F32) + from_p[:, c].astype(F32)).astype(BF16)
         own[0, :, c] = total
         low_part[:, :, c] = dot(p_t[...], total).astype(BF16).reshape(N_FSDP, -1, WIDTHS[j])
-        to_fsdp(lambda to: low_part.at[to, :, c], low_in.at[f, :, c], low_ssem.at[j], low_rsem.at[j])
+        to_fsdp(lambda to: low_part.at[to, :, c], low_in.at[f, :, c], low_ssem.at[j], low_rsem.at[j], j == steps - 1)
 
     def stage_adam(j):
         c = cols[j]
@@ -191,7 +208,7 @@
         wait_bytes(low_in.at[pl.ds(0, N_FSDP - 1), :, c], low_rsem.at[j])
         low = jnp.sum(low_in[:, :, c].astype(F32), axis=0)
         low_all[f, :, c] = low.astype(BF16)
-        to_fsdp(lambda to: low_all.at[f, :, c], low_all.at[f, :, c], all_ssem.at[j], all_rsem.at[j])
+        to_fsdp(lambda to: low_all.at[f, :, c], low_all.at[f, :, c], all_ssem.at[j], all_rsem.at[j], j == steps - 1)
         one = 0.9 * m_buf[:, c] + 0.1 * low
         two = 0.999 * v_buf[:, c] + 0.001 * low * low
         m_buf[:, c] = one
@@ -228,28 +245,34 @@
         start_sib(j)
     for copy in loads[1:]:
         copy.start()
-
-    for t in range(steps + 4):
+    loads[0].wait()
+    p_bf[...] = p_buf[...].astype(BF16)
+    p_t[...] = dot_nt(diagonal((rank, rank), 0, 0).astype(BF16), p_bf[...]).astype(BF16)
+
+    stage_opposite(0)
+    for t in range(steps + 3):
         if t + AHEAD < steps:
             start_loads(t + AHEAD)
             start_sib(t + AHEAD)
+        if t + 1 < steps:
+            stage_opposite(t + 1)
         if t < steps:
             stage_pair(t)
+        if t < steps:
+            stage_pass(t)
         if t == 1:
             for copy in loads[1:]:
                 copy.wait()
         if 1 <= t < steps + 1:
-            stage_pass(t - 1)
+            stage_low(t - 1)
         if 2 <= t < steps + 2:
-            stage_low(t - 2)
-        if 3 <= t < steps + 3:
-            stage_adam(t - 3)
-        if 4 <= t:
-            stage_tangent(t - 4)
-            if t - 4 < NORM_EARLY:
-                stage_norm(t - 4)
-        if 6 <= t < NORM_EARLY + 6:
-            stage_weight(t - 6)
+            stage_adam(t - 2)
+        if 3 <= t:
+            stage_tangent(t - 3)
+            if t - 3 < NORM_EARLY:
+                stage_norm(t - 3)
+        if 5 <= t < NORM_EARLY + 5:
+            stage_weight(t - 5)
 
     tan_send[...] = tan_acc[...].astype(BF16).reshape(N_X, 2, tan_rows, rank)
     pair_copy = remote(tan_send.at[:, 1 - core], tan_sib, tail_ssem.at[0], tail_rsem.at[0], sib)
@@ -301,10 +324,19 @@
             gram_send[at, 16:32] = gram_pt[block].astype(BF16)
             gram_send[at, 32:48] = gram_tt[block].astype(BF16)
             gram_send[at, 48:64] = stats
-    to_fsdp(lambda to: gram_send.at[to], gram_in.at[f], tail_ssem.at[4], tail_rsem.at[4])
+    to_fsdp(lambda to: gram_send.at[to], gram_in.at[f], tail_ssem.at[4], tail_rsem.at[4], True)
     gram_in[f] = gram_send[f]
     for j in range(NORM_EARLY + 2, steps):
         stage_weight(j)
+    for j in range(steps):
+        c = cols[j]
+        for q in range(N_X):
+            sib_copy(q, j).wait_send()
+        for k in range(6):
+            x_copy(k, j).wait_send()
+        wait_bytes(low_in.at[pl.ds(0, N_FSDP - 1), :, c], low_ssem.at[j])
+        wait_bytes(low_all.at[pl.ds(0, N_FSDP - 1), :, c], all_ssem.at[j])
+        wait_bytes(norm_all.at[pl.ds(0, N_FSDP - 1), :, c], norm_ssem.at[j])
     wait_bytes(gram_in.at[pl.ds(0, N_FSDP - 1)], tail_rsem.at[4])
     sums = jnp.sum(gram_in[...].astype(F32), axis=0)
     tan_total = jnp.sum(sums[48:56])
@@ -312,18 +344,27 @@
     tan_scale = 0.5 * jnp.sqrt(F32(rank)) / jnp.sqrt(jnp.full((1, 1), tan_total, F32) + 1e-06)
     middle = (proj_total + tan_scale * tan_scale * tan_total) / rank
     block = sums[0:16] + tan_scale * sums[16:32] + tan_scale * tan_scale * sums[32:48]
-    on_diagonal = diagonal((16, 128), d * tan_rows + (f // 4) * 16, (f % 4) * 128)
+    on_diagonal = diagonal((16, 128), d * tan_rows + y * 16, z * 128)
     gram_all[x, core, f] = (block - jnp.where(on_diagonal, middle, 0.0)).astype(BF16)
     mine = gram_all.at[x, core, f]
 
-    @pl.loop(1, N_CHIPS)
-    def _(i):
-        remote(mine, mine, tail_ssem.at[5], tail_rsem.at[5], chip_at(i)).start()
+    for at in chips:
+        remote(mine, mine, tail_ssem.at[5], tail_rsem.at[5], chip_at(at)).start()
 
     scale_buf[0:8] = jnp.broadcast_to(tan_scale, (8, 128))
     scale_buf[8:16] = jnp.broadcast_to(middle, (8, 128))
     scale_copy = pltpu.make_async_copy(scale_buf, scale_out, out_sem.at[steps + 3])
     scale_copy.start()
+    pair_copy.wait_send()
+    wait_bytes(tan_in.at[pl.ds(0, N_X - 1)], tail_ssem.at[1])
+    wait_bytes(tan_all.at[pl.ds(0, N_X - 1), 0], tail_ssem.at[2])
+    pair_all.wait_send()
+    wait_bytes(gram_in.at[pl.ds(0, N_FSDP - 1)], tail_ssem.at[4])
+    for copy in outs:
+        copy.wait()
+    for j in range(steps):
+        weight_copy(j).wait()
+    tan_copy.wait()
     blocks = own.at[0, pl.ds(0, 144), pl.ds(0, 896)]
     wait_bytes(blocks, tail_rsem.at[5])
     pair_gram = remote(gram_all.at[:, core], gram_all.at[:, core], tail_ssem.at[7], tail_rsem.at[7], sib)
@@ -332,26 +373,8 @@
     gram_copy = pltpu.make_async_copy(gram_all, gram_out, out_sem.at[steps + 4])
     gram_copy.start()
 
-    for j in range(steps):
-        c = cols[j]
-        for q in range(N_X):
-            sib_copy(q, j).wait_send()
-        for k in range(6):
-            x_copy(k, j).wait_send()
-        wait_bytes(low_in.at[pl.ds(0, N_FSDP - 1), :, c], low_ssem.at[j])
-        wait_bytes(low_all.at[pl.ds(0, N_FSDP - 1), :, c], all_ssem.at[j])
-        wait_bytes(norm_all.at[pl.ds(0, N_FSDP - 1), :, c], norm_ssem.at[j])
-        weight_copy(j).wait()
-    pair_copy.wait_send()
-    wait_bytes(tan_in.at[pl.ds(0, N_X - 1)], tail_ssem.at[1])
-    wait_bytes(tan_all.at[pl.ds(0, N_X - 1), 0], tail_ssem.at[2])
-    pair_all.wait_send()
-    wait_bytes(gram_in.at[pl.ds(0, N_FSDP - 1)], tail_ssem.at[4])
     wait_bytes(blocks, tail_ssem.at[5])
     pair_gram.wait_send()
-    for copy in outs:
-        copy.wait()
-    tan_copy.wait()
     scale_copy.wait()
     gram_copy.wait()
 

time: 133 us -> 129 us (0.970)
  Pallas kernels: 132 us -> 128 us
    pallas_call x1, Pallas kernels: 123 us -> 119 us  [on_device(): pl.pallas_call(kernel, out_shape=(shape(weight.shape, weight.dtype), shap...]
where the time goes in v3:
time: 129 us
  Pallas kernels  128 us (99%)
    pallas_call x1, Pallas kernels, on_device(): pl.pallas_call(kernel, out_shape=(shape(weight.shape, weight.dtype), shap...  119 us
    pallas_call x1, Pallas kernels, on_device(): pl.pallas_call(finish_kernel, out_shape=(shape(weight.shape, weight.dtype...  9.27 us

profile of v3, /device:TPU:1, one launch (start us, length us, event | category | flops | bytes accessed | tf_op | source)
XLA Modules:
  0.0 128.8 jit_solution(536376457192001869)
XLA Ops:
  0.6 118.7 %shard_map.84 = (bf16[512,1792]{1,0:T(8,128)(2,1)}, f32[32,1792]{1,0:T(8,128)}, f32[32,1792]{1,0:T(8,128)}, bf16[4,2,64,512]{3,2,1,0:T(8,128)(2,1)}, bf16[4,2,16...) custom-call(bf16[512,14336]{1,0:T(8,128)(2,1)} %bitcast.1, bf16[512,1792]{1,0:T(8,128)(2,1)} %weight.1, f32[512,512]{1,0:T(8,128)} %proj.3, ...), custom_call_target="tpu_custom_call" | custom-call | tf_op jit(solution)/shard_map/pallas_call | solution.py:469
  119.3 9.3 %shard_map.85 = (bf16[512,1792]{1,0:T(8,128)(2,1)}, f32[512,512]{1,0:T(8,128)}, f32[32,1792]{1,0:T(8,128)}, f32[32,1792]{1,0:T(8,128)}) custom-call(bf16[512,1792]{1,0:T(8,128)(2,1)} %get-tuple-element.10.weight_in, f32[32,1792]{1,0:T(8,128)} %get-tuple-element.11.one_in, f32[32,1792]{1,0:T(8,128)} %get-tuple-element.12.two_in, ...), custom_call_target="tpu_custom_call" | custom-call | tf_op jit(solution)/shard_map/pallas_call | solution.py:528

commit v4 on v3

--- a/solution.py
+++ b/solution.py
@@ -22,6 +22,7 @@
 WIDTHS = (256,) * 7
 AHEAD = 2
 NORM_EARLY = 3
+TAN_PARTS = 2
 
 
 def dot(left, right):
@@ -53,9 +54,9 @@
     own, sib_in, opp_top, opp_bot, from_m, from_p,
     low_part, low_in, low_all, norm_all,
     w_buf, p_buf, m_buf, v_buf, p_bf, p_t, tan_acc,
-    tan_send, tan_sib, tan_x, tan_in, tan_all, gram_send, gram_in, gram_all, scale_buf,
+    tan_send, tan_sib, tan_x, tan_in, tan_all, base_send, base_in, proj_pick, gram_send, gram_in, gram_all, scale_buf,
     load_sem, own_sem, sib_ssem, sib_rsem, x_ssem, x_rsem,
-    low_ssem, low_rsem, all_ssem, all_rsem, norm_ssem, norm_rsem, tail_ssem, tail_rsem, out_sem,
+    low_ssem, low_rsem, all_ssem, all_rsem, norm_ssem, norm_rsem, tan_ssem, tan_rsem, tail_ssem, tail_rsem, out_sem,
 ):
     rows = grad.shape[0]
     rank = proj.shape[1]
@@ -239,30 +240,47 @@
         w_buf[:, c] = (w_buf[:, c].astype(F32) - 2.0 * update).astype(BF16)
         weight_copy(j).start()
 
+    pick = diagonal((tan_rows, rank), d * tan_rows, 0).astype(BF16)
+
+    def send_proj_gram():
+        proj_pick[...] = dot_nt(pick, p_bf[...]).astype(BF16)
+        gram_pp = dot(proj_pick[...], p_bf[...])
+        proj_sq = fold_rows(p_buf[...] * p_buf[...])
+        proj_sq = jnp.concatenate([proj_sq, jnp.zeros_like(proj_sq)], axis=0).astype(BF16)
+        for to_y in range(4):
+            for to_z in range(4):
+                block = gram_pp[16 * to_y : 16 * to_y + 16, 128 * to_z : 128 * to_z + 128]
+                base_send[4 * to_y + to_z, 0:16] = block.astype(BF16)
+                base_send[4 * to_y + to_z, 16:32] = proj_sq
+        to_fsdp(lambda to: base_send.at[to], base_in.at[f], tail_ssem.at[6], tail_rsem.at[6])
+        base_in[f] = base_send[f]
+
     start_sib(0)
+    stage_opposite(0)
     for j in range(1, AHEAD):
         start_loads(j)
         start_sib(j)
+    stage_pair(0)
     for copy in loads[1:]:
         copy.start()
     loads[0].wait()
     p_bf[...] = p_buf[...].astype(BF16)
     p_t[...] = dot_nt(diagonal((rank, rank), 0, 0).astype(BF16), p_bf[...]).astype(BF16)
 
-    stage_opposite(0)
     for t in range(steps + 3):
         if t + AHEAD < steps:
             start_loads(t + AHEAD)
             start_sib(t + AHEAD)
         if t + 1 < steps:
             stage_opposite(t + 1)
-        if t < steps:
+        if 0 < t < steps:
             stage_pair(t)
         if t < steps:
             stage_pass(t)
         if t == 1:
             for copy in loads[1:]:
                 copy.wait()
+            send_proj_gram()
         if 1 <= t < steps + 1:
             stage_low(t - 1)
         if 2 <= t < steps + 2:
@@ -277,53 +295,55 @@
     tan_send[...] = tan_acc[...].astype(BF16).reshape(N_X, 2, tan_rows, rank)
     pair_copy = remote(tan_send.at[:, 1 - core], tan_sib, tail_ssem.at[0], tail_rsem.at[0], sib)
     pair_copy.start()
+    stage_norm(NORM_EARLY)
     pair_copy.wait_recv()
-    tan_x[...] = (tan_send[:, core].astype(F32) + tan_sib[...].astype(F32)).astype(BF16)
-    to_x(lambda to: tan_x.at[to], tan_in.at[x], tail_ssem.at[1], tail_rsem.at[1])
-    tan_in[x] = tan_x[x]
-    for j in range(NORM_EARLY, steps):
+    parts = [pl.ds(k * (rank // TAN_PARTS), rank // TAN_PARTS) for k in range(TAN_PARTS)]
+    for k, c in enumerate(parts):
+        tan_x[:, :, c] = (tan_send[:, core, :, c].astype(F32) + tan_sib[:, :, c].astype(F32)).astype(BF16)
+        to_x(lambda to: tan_x.at[to, :, c], tan_in.at[x, :, c], tan_ssem.at[0, k], tan_rsem.at[0, k])
+        tan_in[x, :, c] = tan_x[x, :, c]
+    for j in range(NORM_EARLY + 1, steps - 1):
         stage_norm(j)
+    for k, c in enumerate(parts):
+        wait_bytes(tan_in.at[pl.ds(0, N_X - 1), :, c], tan_rsem.at[0, k])
+        tan_all[x, core, :, c] = jnp.sum(tan_in[:, :, c].astype(F32), axis=0).astype(BF16)
+        mine = tan_all.at[x, core, :, c]
+        to_x(lambda to: mine, mine, tan_ssem.at[1, k], tan_rsem.at[1, k])
+    stage_norm(steps - 1)
     outs = [
         pltpu.make_async_copy(m_buf, moment_one, out_sem.at[steps]),
         pltpu.make_async_copy(v_buf, moment_two, out_sem.at[steps + 1]),
     ]
     for copy in outs:
         copy.start()
-    wait_bytes(tan_in.at[pl.ds(0, N_X - 1)], tail_rsem.at[1])
-    tan_all[x, core] = jnp.sum(tan_in[...].astype(F32), axis=0).astype(BF16)
-    to_x(lambda to: tan_all.at[x, core], tan_all.at[x, core], tail_ssem.at[2], tail_rsem.at[2])
-
     for j in range(NORM_EARLY, NORM_EARLY + 2):
         stage_weight(j)
-    proj_sq = fold_rows(p_buf[...] * p_buf[...])
-    pick = diagonal((tan_rows, rank), d * tan_rows, 0).astype(BF16)
-    proj_pick = dot_nt(pick, p_bf[...]).astype(BF16)
-
-    wait_bytes(tan_all.at[pl.ds(0, N_X - 1), 0], tail_rsem.at[2])
-    pair_all = remote(tan_all.at[:, core], tan_all.at[:, core], tail_ssem.at[3], tail_rsem.at[3], sib)
-    pair_all.start()
-    pair_all.wait_recv()
+    pair_all = []
+    for k, c in enumerate(parts):
+        wait_bytes(tan_all.at[pl.ds(0, N_X - 1), 0, :, c], tan_rsem.at[1, k])
+        mine = tan_all.at[:, core, :, c]
+        pair_all.append(remote(mine, mine, tan_ssem.at[2, k], tan_rsem.at[2, k], sib))
+        pair_all[k].start()
+    for copy in pair_all:
+        copy.wait_recv()
 
     tan = tan_all[...].reshape(rank, rank)
     tan_copy = pltpu.make_async_copy(tan_all, tan_out, out_sem.at[steps + 2])
     tan_copy.start()
     tan_pick = dot_nt(pick, tan).astype(BF16)
-    picks = jnp.concatenate([proj_pick, tan_pick], axis=0)
-    with_proj = dot(picks, p_bf[...])
-    with_tan = dot(picks, tan)
-    gram_pp = with_proj[:tan_rows]
-    gram_pt = with_proj[tan_rows:] + with_tan[:tan_rows]
+    with_tan = dot(jnp.concatenate([proj_pick[...], tan_pick], axis=0), tan)
+    gram_pt = dot(tan_pick, p_bf[...]) + with_tan[:tan_rows]
     gram_tt = with_tan[tan_rows:]
     tan_f = tan.astype(F32)
-    stats = jnp.concatenate([fold_rows(tan_f * tan_f), proj_sq], axis=0).astype(BF16)
+    tan_sq = fold_rows(tan_f * tan_f)
+    stats = jnp.concatenate([tan_sq, jnp.zeros_like(tan_sq)], axis=0).astype(BF16)
     for to_y in range(4):
         for to_z in range(4):
             block = (slice(16 * to_y, 16 * to_y + 16), slice(128 * to_z, 128 * to_z + 128))
             at = 4 * to_y + to_z
-            gram_send[at, 0:16] = gram_pp[block].astype(BF16)
-            gram_send[at, 16:32] = gram_pt[block].astype(BF16)
-            gram_send[at, 32:48] = gram_tt[block].astype(BF16)
-            gram_send[at, 48:64] = stats
+            gram_send[at, 0:16] = gram_pt[block].astype(BF16)
+            gram_send[at, 16:32] = gram_tt[block].astype(BF16)
+            gram_send[at, 32:48] = stats
     to_fsdp(lambda to: gram_send.at[to], gram_in.at[f], tail_ssem.at[4], tail_rsem.at[4], True)
     gram_in[f] = gram_send[f]
     for j in range(NORM_EARLY + 2, steps):
@@ -337,13 +357,15 @@
         wait_bytes(low_in.at[pl.ds(0, N_FSDP - 1), :, c], low_ssem.at[j])
         wait_bytes(low_all.at[pl.ds(0, N_FSDP - 1), :, c], all_ssem.at[j])
         wait_bytes(norm_all.at[pl.ds(0, N_FSDP - 1), :, c], norm_ssem.at[j])
+    wait_bytes(base_in.at[pl.ds(0, N_FSDP - 1)], tail_rsem.at[6])
+    base = jnp.sum(base_in[...].astype(F32), axis=0)
+    proj_total = jnp.sum(base[16:32])
     wait_bytes(gram_in.at[pl.ds(0, N_FSDP - 1)], tail_rsem.at[4])
     sums = jnp.sum(gram_in[...].astype(F32), axis=0)
-    tan_total = jnp.sum(sums[48:56])
-    proj_total = jnp.sum(sums[56:64])
+    tan_total = jnp.sum(sums[32:40])
     tan_scale = 0.5 * jnp.sqrt(F32(rank)) / jnp.sqrt(jnp.full((1, 1), tan_total, F32) + 1e-06)
     middle = (proj_total + tan_scale * tan_scale * tan_total) / rank
-    block = sums[0:16] + tan_scale * sums[16:32] + tan_scale * tan_scale * sums[32:48]
+    block = base[0:16] + tan_scale * sums[0:16] + tan_scale * tan_scale * sums[16:32]
     on_diagonal = diagonal((16, 128), d * tan_rows + y * 16, z * 128)
     gram_all[x, core, f] = (block - jnp.where(on_diagonal, middle, 0.0)).astype(BF16)
     mine = gram_all.at[x, core, f]
@@ -355,10 +377,12 @@
     scale_buf[8:16] = jnp.broadcast_to(middle, (8, 128))
     scale_copy = pltpu.make_async_copy(scale_buf, scale_out, out_sem.at[steps + 3])
     scale_copy.start()
+    wait_bytes(base_in.at[pl.ds(0, N_FSDP - 1)], tail_ssem.at[6])
     pair_copy.wait_send()
-    wait_bytes(tan_in.at[pl.ds(0, N_X - 1)], tail_ssem.at[1])
-    wait_bytes(tan_all.at[pl.ds(0, N_X - 1), 0], tail_ssem.at[2])
-    pair_all.wait_send()
+    for k, c in enumerate(parts):
+        wait_bytes(tan_in.at[pl.ds(0, N_X - 1), :, c], tan_ssem.at[0, k])
+        wait_bytes(tan_all.at[pl.ds(0, N_X - 1), 0, :, c], tan_ssem.at[1, k])
+        pair_all[k].wait_send()
     wait_bytes(gram_in.at[pl.ds(0, N_FSDP - 1)], tail_ssem.at[4])
     for copy in outs:
         copy.wait()
@@ -429,7 +453,7 @@
             q_now = q_state[...]
             q_state[...] = q_center * poly + poly_center * q_now + dot(q_now.astype(BF16), poly_b)
             q_center = q_center * poly_center
-        if sweep == 0:
+        if sweep == 1:
             for copy, on in zip(copies[4:], passed):
                 copy.wait()
                 on.start()
@@ -444,13 +468,19 @@
     copies[2].wait()
     copies[3].wait()
     scale_down = 1.0 / jnp.sqrt(frame_sq)
-    frame = (proj_buf[...] + tan_scale * tan_buf[...].reshape(rank, rank).astype(F32)) * scale_down
-    out_buf[...] = (q_center + q_shift) * frame + dot(frame.astype(BF16), q_b)
-    last = pltpu.make_async_copy(out_buf, new_proj, sems.at[7])
-    last.start()
+    q_all = q_center + q_shift
+    last = []
+    part = proj_buf.shape[0] // N_X
+    for k in range(N_X):
+        at = pl.ds(k * part, part)
+        frame = (proj_buf[at] + tan_scale * tan_buf[k].reshape(part, rank).astype(F32)) * scale_down
+        out_buf[at] = q_all * frame + dot(frame.astype(BF16), q_b)
+        last.append(pltpu.make_async_copy(out_buf.at[at], new_proj.at[at], sems.at[7 + k]))
+        last[k].start()
     for copy in passed:
         copy.wait()
-    last.wait()
+    for copy in last:
+        copy.wait()
 
 
 def on_device(grad_parts, weight, projector, exp_avg, exp_avg_sq):
@@ -501,8 +531,11 @@
             vmem((N_X, tan_rows, rank), BF16),
             vmem((N_X, tan_rows, rank), BF16),
             vmem(tan_shape, BF16),
-            vmem((N_FSDP, 64, 128), BF16),
-            vmem((N_FSDP, 64, 128), BF16),
+            vmem((N_FSDP, 32, 128), BF16),
+            vmem((N_FSDP, 32, 128), BF16),
+            vmem((tan_rows, rank), BF16),
+            vmem((N_FSDP, 48, 128), BF16),
+            vmem((N_FSDP, 48, 128), BF16),
             vmem(gram_shape, BF16),
             vmem((16, 128), F32),
             dma((4,)),
@@ -517,6 +550,8 @@
             dma((steps,)),
             dma((steps,)),
             dma((steps,)),
+            dma((3, TAN_PARTS)),
+            dma((3, TAN_PARTS)),
             dma((8,)),
             dma((8,)),
             dma((steps + 5,)),
@@ -546,7 +581,7 @@
             vmem(weight.shape, BF16),
             vmem(exp_avg.shape, F32),
             vmem(exp_avg_sq.shape, F32),
-            dma((8,)),
+            dma((11,)),
         ],
         compiler_params=pltpu.CompilerParams(vmem_limit_bytes=60 * 1024 * 1024),
     )(*mid, projector)

time: 129 us -> 126 us (0.977)
  Pallas kernels: 128 us -> 125 us
    pallas_call x1, Pallas kernels: 119 us -> 117 us  [on_device(): pl.pallas_call(kernel, out_shape=(shape(weight.shape, weight.dtype), shap...]
where the time goes in v4:
time: 126 us
  Pallas kernels  125 us (99%)
    pallas_call x1, Pallas kernels, on_device(): pl.pallas_call(kernel, out_shape=(shape(weight.shape, weight.dtype), shap...  117 us
    pallas_call x1, Pallas kernels, on_device(): pl.pallas_call(finish_kernel, out_shape=(shape(weight.shape, weight.dtype...  8.7 us

profile of v4, /device:TPU:1, one launch (start us, length us, event | category | flops | bytes accessed | tf_op | source)
XLA Modules:
  0.0 126.2 jit_solution(8761944627249936469)
XLA Ops:
  0.6 116.7 %shard_map.84 = (bf16[512,1792]{1,0:T(8,128)(2,1)}, f32[32,1792]{1,0:T(8,128)}, f32[32,1792]{1,0:T(8,128)}, bf16[4,2,64,512]{3,2,1,0:T(8,128)(2,1)}, bf16[4,2,16...) custom-call(bf16[512,14336]{1,0:T(8,128)(2,1)} %bitcast.1, bf16[512,1792]{1,0:T(8,128)(2,1)} %weight.1, f32[512,512]{1,0:T(8,128)} %proj.3, ...), custom_call_target="tpu_custom_call" | custom-call | tf_op jit(solution)/shard_map/pallas_call | solution.py:499
  117.4 8.7 %shard_map.85 = (bf16[512,1792]{1,0:T(8,128)(2,1)}, f32[512,512]{1,0:T(8,128)}, f32[32,1792]{1,0:T(8,128)}, f32[32,1792]{1,0:T(8,128)}) custom-call(bf16[512,1792]{1,0:T(8,128)(2,1)} %get-tuple-element.10.weight_in, f32[32,1792]{1,0:T(8,128)} %get-tuple-element.11.one_in, f32[32,1792]{1,0:T(8,128)} %get-tuple-element.12.two_in, ...), custom_call_target="tpu_custom_call" | custom-call | tf_op jit(solution)/shard_map/pallas_call | solution.py:563

commit v5 on v4

--- a/solution.py
+++ b/solution.py
@@ -22,7 +22,7 @@
 WIDTHS = (256,) * 7
 AHEAD = 2
 NORM_EARLY = 3
-TAN_PARTS = 2
+TAN_PARTS = 4
 
 
 def dot(left, right):
@@ -193,6 +193,12 @@
         own[3, bot, c] = (own[3, bot, c].astype(F32) + opp_bot[:, c].astype(F32)).astype(BF16)
         x_copy(5, j).start()
 
+    def pieces(j):
+        if j < steps - 1:
+            return [(cols[j], j)]
+        part = WIDTHS[j] // 2
+        return [(pl.ds(starts[j], part), j), (pl.ds(starts[j] + part, part), steps)]
+
     def stage_low(j):
         c = cols[j]
         total = pair_sum(0, j)
@@ -201,34 +207,39 @@
         total = (total + from_m[:, c].astype(F32) + from_p[:, c].astype(F32)).astype(BF16)
         own[0, :, c] = total
         low_part[:, :, c] = dot(p_t[...], total).astype(BF16).reshape(N_FSDP, -1, WIDTHS[j])
-        to_fsdp(lambda to: low_part.at[to, :, c], low_in.at[f, :, c], low_ssem.at[j], low_rsem.at[j], j == steps - 1)
+        for c, k in pieces(j):
+            to_fsdp(lambda to: low_part.at[to, :, c], low_in.at[f, :, c], low_ssem.at[k], low_rsem.at[k])
 
     def stage_adam(j):
-        c = cols[j]
-        low_in[f, :, c] = low_part[f, :, c]
-        wait_bytes(low_in.at[pl.ds(0, N_FSDP - 1), :, c], low_rsem.at[j])
-        low = jnp.sum(low_in[:, :, c].astype(F32), axis=0)
-        low_all[f, :, c] = low.astype(BF16)
-        to_fsdp(lambda to: low_all.at[f, :, c], low_all.at[f, :, c], all_ssem.at[j], all_rsem.at[j], j == steps - 1)
-        one = 0.9 * m_buf[:, c] + 0.1 * low
-        two = 0.999 * v_buf[:, c] + 0.001 * low * low
-        m_buf[:, c] = one
-        v_buf[:, c] = two
-        norm_all[f, :, c] = (one / (jnp.sqrt(two) + 1e-08)).astype(BF16)
+        low_in[f, :, cols[j]] = low_part[f, :, cols[j]]
+        lows = []
+        for c, k in pieces(j):
+            wait_bytes(low_in.at[pl.ds(0, N_FSDP - 1), :, c], low_rsem.at[k])
+            low = jnp.sum(low_in[:, :, c].astype(F32), axis=0)
+            low_all[f, :, c] = low.astype(BF16)
+            mine = low_all.at[f, :, c]
+            to_fsdp(lambda to: mine, mine, all_ssem.at[k], all_rsem.at[k])
+            lows.append(low)
+        for low, (c, k) in zip(lows, pieces(j)):
+            one = 0.9 * m_buf[:, c] + 0.1 * low
+            two = 0.999 * v_buf[:, c] + 0.001 * low * low
+            m_buf[:, c] = one
+            v_buf[:, c] = two
+            norm_all[f, :, c] = (one / (jnp.sqrt(two) + 1e-08)).astype(BF16)
 
     def stage_norm(j):
         c = cols[j]
         to_fsdp(lambda to: norm_all.at[f, :, c], norm_all.at[f, :, c], norm_ssem.at[j], norm_rsem.at[j])
 
     def stage_tangent(j):
-        c = cols[j]
-        wait_bytes(low_all.at[pl.ds(0, N_FSDP - 1), :, c], all_rsem.at[j])
-        low = low_all[:, :, c].reshape(rank, WIDTHS[j])
-        resid = (own[0, :, c].astype(F32) - dot(p_bf[...], low)).astype(BF16)
-        if j == 0:
-            tan_acc[...] = dot_nt(resid, low)
-        else:
-            tan_acc[...] += dot_nt(resid, low)
+        for c, k in pieces(j):
+            wait_bytes(low_all.at[pl.ds(0, N_FSDP - 1), :, c], all_rsem.at[k])
+            low = low_all[:, :, c].reshape(rank, c.size)
+            resid = (own[0, :, c].astype(F32) - dot(p_bf[...], low)).astype(BF16)
+            if j == 0:
+                tan_acc[...] = dot_nt(resid, low)
+            else:
+                tan_acc[...] += dot_nt(resid, low)
 
     def weight_copy(j):
         return pltpu.make_async_copy(w_buf.at[:, cols[j]], new_weight.at[:, cols[j]], out_sem.at[j])
@@ -354,8 +365,9 @@
             sib_copy(q, j).wait_send()
         for k in range(6):
             x_copy(k, j).wait_send()
-        wait_bytes(low_in.at[pl.ds(0, N_FSDP - 1), :, c], low_ssem.at[j])
-        wait_bytes(low_all.at[pl.ds(0, N_FSDP - 1), :, c], all_ssem.at[j])
+        for part, k in pieces(j):
+            wait_bytes(low_in.at[pl.ds(0, N_FSDP - 1), :, part], low_ssem.at[k])
+            wait_bytes(low_all.at[pl.ds(0, N_FSDP - 1), :, part], all_ssem.at[k])
         wait_bytes(norm_all.at[pl.ds(0, N_FSDP - 1), :, c], norm_ssem.at[j])
     wait_bytes(base_in.at[pl.ds(0, N_FSDP - 1)], tail_rsem.at[6])
     base = jnp.sum(base_in[...].astype(F32), axis=0)
@@ -544,10 +556,10 @@
             dma((steps, N_X)),
             dma((steps, 6)),
             dma((steps, 6)),
-            dma((steps,)),
-            dma((steps,)),
-            dma((steps,)),
-            dma((steps,)),
+            dma((steps + 1,)),
+            dma((steps + 1,)),
+            dma((steps + 1,)),
+            dma((steps + 1,)),
             dma((steps,)),
             dma((steps,)),
             dma((3, TAN_PARTS)),

time: 126 us -> 126 us (level)
  no operation moved by 1% of the time
where the time goes in v5:
time: 126 us
  Pallas kernels  125 us (99%)
    pallas_call x1, Pallas kernels, on_device(): pl.pallas_call(kernel, out_shape=(shape(weight.shape, weight.dtype), shap...  116 us
    pallas_call x1, Pallas kernels, on_device(): pl.pallas_call(finish_kernel, out_shape=(shape(weight.shape, weight.dtype...  8.69 us

profile of v5, /device:TPU:1, one launch (start us, length us, event | category | flops | bytes accessed | tf_op | source)
XLA Modules:
  0.0 125.9 jit_solution(6572241252821742764)
XLA Ops:
  0.6 116.4 %shard_map.84 = (bf16[512,1792]{1,0:T(8,128)(2,1)}, f32[32,1792]{1,0:T(8,128)}, f32[32,1792]{1,0:T(8,128)}, bf16[4,2,64,512]{3,2,1,0:T(8,128)(2,1)}, bf16[4,2,16...) custom-call(bf16[512,14336]{1,0:T(8,128)(2,1)} %bitcast.1, bf16[512,1792]{1,0:T(8,128)(2,1)} %weight.1, f32[512,512]{1,0:T(8,128)} %proj.3, ...), custom_call_target="tpu_custom_call" | custom-call | tf_op jit(solution)/shard_map/pallas_call | solution.py:511
  117.0 8.7 %shard_map.85 = (bf16[512,1792]{1,0:T(8,128)(2,1)}, f32[512,512]{1,0:T(8,128)}, f32[32,1792]{1,0:T(8,128)}, f32[32,1792]{1,0:T(8,128)}) custom-call(bf16[512,1792]{1,0:T(8,128)(2,1)} %get-tuple-element.10.weight_in, f32[32,1792]{1,0:T(8,128)} %get-tuple-element.11.one_in, f32[32,1792]{1,0:T(8,128)} %get-tuple-element.12.two_in, ...), custom_call_target="tpu_custom_call" | custom-call | tf_op jit(solution)/shard_map/pallas_call | solution.py:575
